TPU v7x, 256 devices: a whole 4x4x8 slice. The times are simulated.
256 devices in a mesh: row: 2 (over x_hi), col: 64 (over z, y, core), sk: 2 (over x_lo).
Axes of the slice: x: 4 (x_hi: 2, x_lo: 2; x = x_hi * 2 + x_lo), y: 4, z: 8, core: 2. Of those that a mesh axis runs over, the one named last changes fastest.
Arguments:
- tiles: bfloat16 [2, 64, 4, 1024, 1024], P('row', 'col'), may hold values from -0.09375 to 0.09375
- tile_rows: int32 [2, 64, 4], P('row', 'col'), may hold values from 0 to 1, as said below
- tile_cols: int32 [2, 64, 4], P('row', 'col'), may hold values from 0 to 1, as said below
- tile_count: int32 [2, 64], P('row', 'col'), may hold values from 1 to 4, as said below
- sketch: bfloat16 [131072, 512], P('col', 'sk'), may hold values from -6 to 6
Outputs:
- basis: float32 [131072, 512], P('col', 'sk')
- factor: float32 [512, 512], replicated
Inputs may be any that keep to these rules, and one draw needn't show every extreme that they name: `tile_rows`: within one pair of slabs the slots name distinct (row, column) tile positions. `tile_cols`: within one pair of slabs the slots name distinct (row, column) tile positions. `tile_count`: some pair of slabs has all 4 slots live.
All inputs are finite; a program needn't handle non-finite values.
Results may differ from a plain program's by a relative error of at most 0.0031.
Values sent between devices are 32-bit elements; how exact they have to be, the bound alone decides.
No kernel may reach another device: no remote copies, remote signals or barrier semaphores. Data moves between devices by JAX's collectives and lax.ppermute only.
A program may use at most 64 MiB of HBM per device.

v0:
```python
import jax
import jax.numpy as jnp
from jax import lax
from jax.sharding import PartitionSpec as P

RB = 2


def slab_product(blocks, sources, pick, place, count, groups, flip):
    high = lax.Precision.HIGHEST
    picked = sources[pick]
    form = "sji,sjk->sik" if flip else "sij,sjk->sik"
    prod = jnp.einsum(form, blocks, picked, preferred_element_type=jnp.float32)
    live = (jnp.arange(blocks.shape[0]) < count).astype(jnp.float32)
    weights = (place[:, None] == jnp.arange(groups)[None, :]).astype(jnp.float32) * live[:, None]
    return jnp.einsum("sg,sik->gik", weights, prod, precision=high)


def on_device(tiles, tile_rows, tile_cols, tile_count, sketch):
    high = lax.Precision.HIGHEST
    blocks = tiles[0, 0]
    rows = tile_rows[0, 0]
    cols = tile_cols[0, 0]
    count = tile_count[0, 0]
    tb = blocks.shape[1]
    narrow = sketch.shape[1]
    nblock = sketch.shape[0] // tb
    sketch_blocks = sketch.reshape(nblock, tb, narrow)
    partial_y = slab_product(blocks, sketch_blocks, cols, rows, count, RB, False)
    summed_y = lax.psum(partial_y, "col")
    slab_y = (summed_y * 0.75).astype(jnp.bfloat16)
    partial_z = slab_product(blocks, slab_y, rows, cols, count, nblock, True).reshape(
        nblock * tb, narrow
    )
    total_rows = nblock * tb * lax.axis_size("col")
    width = narrow * lax.axis_size("sk")
    start = lax.axis_index("sk") * narrow
    slab_z = lax.psum(partial_z, "row")
    wide_z = lax.all_gather(slab_z, "sk", axis=1, tiled=True)
    gram = jnp.dot(wide_z.T, wide_z, precision=high, preferred_element_type=jnp.float32)
    gram = lax.psum(gram, "col") / total_rows
    lower = jnp.linalg.cholesky(gram)
    inverse = jax.scipy.linalg.solve_triangular(
        lower, jnp.eye(width, dtype=jnp.float32), lower=True
    )
    own = lax.dynamic_slice_in_dim(inverse, start, narrow, 0)
    basis = jnp.dot(wide_z, own.T, precision=high, preferred_element_type=jnp.float32)
    return (basis, lower.T)


def solution(mesh):
    return jax.shard_map(
        on_device,
        mesh=mesh,
        in_specs=(
            P("row", "col", None, None, None),
            P("row", "col", None),
            P("row", "col", None),
            P("row", "col"),
            P("col", "sk"),
        ),
        out_specs=(P("col", "sk"), P()),
        check_vma=False,
    )
```

profile of v0, /device:TPU:2, one launch (start us, length us, event | category | flops | bytes accessed | tf_op | source)
XLA Modules:
  0.0 760.7 jit_solution(8993457495748163062)
XLA Ops:
  8.0 0.7 fusion.53
  8.6 0.7 gather_fusion
  9.3 7.8 %fusion.6 = f32[4,1024,256]{1,2,0:T(8,128)} fusion(bf16[4,1024,256]{2,1,0:T(8,128)(2,1)S(1)} %gather_fusion, bf16[1,1,4,1024,1024]{4,3,2,1,0:T(8,128)(2,1)} %param.5), kind=kOutput, calls=%fused_computation.10 | convolution fusion | flops 2147483648 | bytes 14680064 | tf_op jit(solution)/shard_map/sij,sjk->sik/dot_general | solution.py:13
  17.1 5.2 copy.14
  22.4 9.2 %fusion.49 = f32[2,1024,256]{2,0,1:T(2,128)S(1)} fusion(f32[4,1024,256]{2,0,1:T(4,128)} %copy.14, s32[4]{0:T(128)S(1)} %bitcast.90, f32[4]{0:T(128)S(1)} %compare_convert_fusion), kind=kOutput, calls=%fused_computation.92 | convolution fusion | flops 25165840 | bytes 6291488 | tf_op jit(solution)/shard_map/sg,sik->gik/dot_general | solution.py:16
  31.6 1.5 copy.15
  33.1 0.5 all-reduce.7.cloned.1.call-start
  33.7 192.0 %all-reduce.5.cloned.1.call-done = f32[2,1024,256]{2,1,0:T(8,128)} async-done(((f32[2,1024,256]{2,1,0:T(8,128)}), f32[2,1024,256]{2,1,0:T(8,128)}) %all-reduce.5.cloned.1.call-update) | async-done | bytes 2097168 | tf_op jit(solution)/shard_map/psum | solution.py:30
  225.6 1.8 multiply_convert_fusion
  227.4 2.0 gather_fusion.1
  229.4 8.3 %fusion = f32[4,256,1024]{2,1,0:T(8,128)} fusion(bf16[4,1024,256]{2,1,0:T(8,128)(2,1)} %gather_fusion.1, bf16[1,1,4,1024,1024]{4,3,2,1,0:T(8,128)(2,1)} %param.5), kind=kOutput, calls=%fused_computation.4 | convolution fusion | flops 2147483648 | bytes 14680064 | tf_op jit(solution)/shard_map/sji,sjk->sik/dot_general | solution.py:13
  237.7 5.2 copy.16
  243.0 9.2 %fusion.4 = f32[2,1024,256]{2,0,1:T(2,128)S(1)} fusion(f32[4,256,1024]{1,0,2:T(4,128)} %copy.16, f32[4]{0:T(128)S(1)} %compare_convert_fusion, s32[4]{0:T(128)S(1)} %bitcast.91), kind=kOutput, calls=%fused_computation.8 | convolution fusion | flops 25165840 | bytes 6291488 | tf_op jit(solution)/shard_map/sg,sik->gik/dot_general | solution.py:16
  252.2 1.5 copy.10
  253.8 74.0 %all-reduce.7.cloned.1.call-done = f32[2048,256]{1,0:T(8,128)} async-done(((f32[2048,256]{1,0:T(8,128)}), f32[2048,256]{1,0:T(8,128)}) %all-reduce.7.cloned.1.call-update) | async-done | bytes 2097168 | tf_op jit(solution)/shard_map/psum | solution.py:38
  327.9 63.0 %all-gather.2.cloned.1.call-done = f32[2048,512]{1,0:T(8,128)} async-done(((f32[2048,256]{1,0:T(8,128)}), f32[2048,512]{1,0:T(8,128)}) %all-gather.2.cloned.1.call-update) | async-done | bytes 4194320 | tf_op jit(solution)/shard_map/all_gather | solution.py:39
  390.8 11.6 %fusion.67 = f32[512,512]{0,1:T(8,128)} fusion(f32[2048,512]{1,0:T(8,128)} %all-gather.2.cloned.1.call-done), kind=kOutput, calls=%fused_computation.113 | convolution fusion | flops 6442450944 | bytes 5242880 | tf_op jit(solution)/shard_map/dot_general | solution.py:40
  402.4 0.1 iota_compare_fusion
  402.5 1.1 fusion.25
  403.6 186.4 %all-reduce.9.cloned.1.call-done = f32[512,512]{0,1:T(8,128)} async-done(((f32[512,512]{0,1:T(8,128)}), f32[512,512]{0,1:T(8,128)}) %all-reduce.9.cloned.1.call-update) | async-done | bytes 1048592 | tf_op jit(solution)/shard_map/psum | solution.py:41
  590.1 2.4 broadcast_multiply_fusion
  592.4 1.6 copy.12
  594.0 0.2 fusion.9
  594.3 1.0 copy-done.2
  595.2 11.7 %cholesky.104 = f32[128,128]{1,0:T(8,128)S(1)} custom-call(f32[128,128]{1,0:T(8,128)S(1)} %cholesky.266), custom_call_target="Cholesky" | custom-call | tf_op jit(solution)/shard_map/jit(cholesky)/cholesky | solution.py:42
  607.0 9.8 %custom-call.31 = f32[1,128,128]{1,2,0:T(8,128)S(1)} custom-call(f32[1,128,128]{2,1,0:T(8,128)S(1)} %get-tuple-element.35), custom_call_target="InvertDiagBlocksLowerTriangular" | custom-call | tf_op jit(solution)/shard_map/jit(cholesky)/cholesky | solution.py:42
  616.8 0.1 cholesky.224
  616.9 1.2 constant_dynamic-update-slice_fusion
  618.2 1.3 convolution_subtract_fusion.3
  619.4 11.7 %cholesky.217 = f32[128,128]{1,0:T(8,128)S(1)} custom-call(f32[128,128]{1,0:T(8,128)S(1)} %cholesky.270), custom_call_target="Cholesky" | custom-call | tf_op jit(solution)/shard_map/jit(cholesky)/cholesky | solution.py:42
  631.2 10.0 %custom-call.32 = f32[1,128,128]{1,2,0:T(8,128)S(1)} custom-call(f32[1,128,128]{2,1,0:T(8,128)S(1)} %get-tuple-element.32), custom_call_target="InvertDiagBlocksLowerTriangular" | custom-call | tf_op jit(solution)/shard_map/jit(cholesky)/cholesky | solution.py:42
  641.2 0.3 convolution_dynamic-update-slice_fusion
  641.4 1.3 convolution_subtract_fusion.4
  642.7 11.7 %cholesky.238 = f32[128,128]{1,0:T(8,128)S(1)} custom-call(f32[128,128]{1,0:T(8,128)S(1)} %cholesky.275), custom_call_target="Cholesky" | custom-call | tf_op jit(solution)/shard_map/jit(cholesky)/cholesky | solution.py:42
  654.5 0.7 compare_reduce_fusion.1
  655.1 9.8 %custom-call.33 = f32[1,128,128]{1,2,0:T(8,128)S(1)} custom-call(f32[1,128,128]{2,1,0:T(8,128)S(1)} %get-tuple-element.29), custom_call_target="InvertDiagBlocksLowerTriangular" | custom-call | tf_op jit(solution)/shard_map/jit(cholesky)/cholesky | solution.py:42
  664.9 0.2 convolution_dynamic-update-slice_fusion.1
  665.2 1.2 convolution_subtract_fusion.5
  666.4 11.9 %cholesky.255 = f32[128,128]{1,0:T(8,128)S(1)} custom-call(f32[128,128]{1,0:T(8,128)S(1)} %convolution_subtract_fusion.5), custom_call_target="Cholesky" | custom-call | tf_op jit(solution)/shard_map/jit(cholesky)/cholesky | solution.py:42
  678.4 0.7 compare_reduce_fusion
  679.0 0.7 compare_reduce_fusion.2
  682.3 1.2 fusion.11
  683.6 13.8 %while.1 = (s32[]{:T(128)}, f32[512,512]{1,0:T(8,128)}, s32[4,2]{0,1:T(2,128)S(1)}, f32[4,128,128]{2,1,0:T(8,128)}, s32[]{:T(128)}) while((s32[]{:T(128)}, f32[512,512]{1,0:T(8,128)}, s32[4,2]{0,1:T(2,128)S(1)}, f32[4,128,128]{2,1,0:T(8,128)}, s32[]{:T(128)}) %tuple.34), condition=%wide.while_cond, body=%wide.while_body.sunk | while | flops 2 | bytes 132705 | solution.py:43
  683.6 0.1 constant_dynamic-slice_fusion.2
  683.6 0.5 fusion.80
  684.2 2.8 bitcast_dynamic-update-slice_fusion.2
  687.0 0.1 constant_dynamic-slice_fusion.2
  687.1 0.5 fusion.80
  687.6 2.8 bitcast_dynamic-update-slice_fusion.2
  690.5 0.1 constant_dynamic-slice_fusion.2
  690.6 0.5 fusion.80
  691.1 2.8 bitcast_dynamic-update-slice_fusion.2
  694.0 0.5 fusion.80
  694.6 2.8 bitcast_dynamic-update-slice_fusion.2
  697.3 40.1 %custom-call.34 = f32[4,128,128]{1,2,0:T(8,128)S(1)} custom-call(f32[4,128,128]{2,1,0:T(8,128)} %get-tuple-element.9), custom_call_target="InvertDiagBlocksLowerTriangular" | custom-call | tf_op jit(solution)/shard_map/jit(_solve_triangular)/triangular_solve | solution.py:43
  737.5 0.3 fusion.27
  737.8 1.4 convolution_subtract_fusion.1
  739.2 0.4 fusion.39
  739.6 1.4 convolution_subtract_fusion
  741.1 1.3 fusion.37
  742.3 1.7 convolution_subtract_fusion.2
  744.0 1.3 fusion.36
  745.3 1.3 copy.13
  746.6 7.1 fusion.20
  (33 shorter events, 0.5 us)
Async XLA Ops:
  7.2 1.5 copy-start
  7.2 218.5 %all-reduce.5.cloned.1.call-start = ((), (), s32[]{:S(2)}) async-start(), calls=%async_computation | async-start | bytes 4194304 | tf_op jit(solution)/shard_map/psum | solution.py:30
  17.1 5.2 copy-start.4
  33.1 294.7 %all-reduce.7.cloned.1.call-start = ((), (), s32[]{:S(2)}) async-start(), calls=%async_computation.1 | async-start | bytes 4194304 | tf_op jit(solution)/shard_map/psum | solution.py:38
  237.7 5.2 copy-start.5
  253.7 137.1 %all-gather.2.cloned.1.call-start = ((), (), s32[]{:S(2)}) async-start(), calls=%async_computation.2 | async-start | bytes 6291456 | tf_op jit(solution)/shard_map/all_gather | solution.py:39
  327.8 262.2 %all-reduce.9.cloned.1.call-start = ((), (), s32[]{:S(2)}) async-start(), calls=%async_computation.3 | async-start | bytes 2097152 | tf_op jit(solution)/shard_map/psum | solution.py:41
  590.1 3.9 copy-start.1
  594.2 1.0 copy-start.2
  737.5 1.7 copy-start.3
Sparse Core Ops, SparseCore 0:
  33.2 192.3 all-reduce.4
  253.8 73.9 all-reduce.6
  329.8 61.0 all-gather.1
  402.5 187.4 all-reduce.8
where the time goes:
time: 767 us; the launch traced here: 761 us
  waiting for transfers between devices  515 us (67%)
  other arithmetic  126 us (16%)
  matrix products  66.5 us (9%)
  local copies, waits for them, and re-layouts  33.9 us (4%)
  between operations  17.8 us (2%)
    psum x1, waiting for transfers between devices, on_device(): summed_y = lax.psum(partial_y, 'col')  192 us
    psum x1, waiting for transfers between devices, on_device(): gram = lax.psum(gram, 'col') / total_rows  186 us
    another operation x14, other arithmetic, on_device(): lower = jnp.linalg.cholesky(gram)  78.8 us
    psum x1, waiting for transfers between devices, on_device(): slab_z = lax.psum(partial_z, 'row')  74 us
    all_gather x1, waiting for transfers between devices, on_device(): wide_z = lax.all_gather(slab_z, 'sk', axis=1, tiled=True)  63 us
    another operation x2, other arithmetic, on_device(): jax.scipy.linalg.solve_triangular(lower, jnp.eye(width, dtype=jnp.float32...  40.1 us
    dot_general x2, matrix products, slab_product(): return jnp.einsum('sg,sik->gik', weights, prod, precision=high)  18.4 us
    dot_general x2, matrix products, slab_product(): prod = jnp.einsum(form, blocks, picked, preferred_element_type=jnp.float32)  16.1 us
  transfers between devices with their start and end apart: 4, of which 4 were waited for; matrix products, arithmetic and copies ran while one was open for 0% of the time, Pallas kernels for 0%

commit v1 on v0

v1 whole, which is shorter than its diff:
```python
import functools

import jax
import jax.numpy as jnp
from jax import lax
from jax.experimental import pallas as pl
from jax.experimental.pallas import tpu as pltpu
from jax.sharding import Mesh, PartitionSpec as P

HIGH = lax.Precision.HIGHEST
F32 = jnp.float32
BF16 = jnp.bfloat16
PLANE = ("z", "y")
RING = ("row", "sk")
SHEET = ("row", "y", "sk")
LIMIT = 48 * 1024 * 1024
SIDE = 128
GROUP = 8
SUB = 32


def dot(a, b, dims, precision=None):
    return lax.dot_general(a, b, (dims, ((), ())), precision=precision, preferred_element_type=F32)


def tile_spec(tb, parts):
    def place(s, i, rows, cols, count):
        live = s < count[0]
        return (jnp.where(live, s, count[0] - 1), jnp.where(live, i, parts - 1), 0)

    return pl.BlockSpec((None, tb // parts, tb), place)


def forward_kernel(parts, rows, cols, count, tiles, sketch, keep, send):
    s = pl.program_id(0)
    i = pl.program_id(1)
    core = lax.axis_index("core")
    depth = tiles.shape[0]

    @pl.when((s == 0) & (i == 0))
    def _():
        keep[...] = jnp.zeros_like(keep)
        send[...] = jnp.zeros_like(send)

    @pl.when(s < count[0])
    def _():
        prod = dot(tiles[...], sketch[cols[s]], ((1,), (0,)))
        here = pl.ds(pl.multiple_of(i * depth, depth), depth)

        @pl.when(rows[s] == core)
        def _():
            keep[here, :] += prod

        @pl.when(rows[s] != core)
        def _():
            send[here, :] += prod


def forward(rows, cols, count, tiles, sketch):
    slots, tb, _ = tiles.shape
    width = sketch.shape[-1]
    parts = 2
    half = jax.ShapeDtypeStruct((tb, width), F32)
    whole = pl.BlockSpec((tb, width), lambda s, i, *_: (0, 0))
    return pl.pallas_call(
        functools.partial(forward_kernel, parts),
        grid_spec=pltpu.PrefetchScalarGridSpec(
            num_scalar_prefetch=3,
            grid=(slots, parts),
            in_specs=[tile_spec(tb, parts), pl.BlockSpec(sketch.shape, lambda s, i, *_: (0, 0, 0))],
            out_specs=[whole, whole],
        ),
        out_shape=[half, half],
        compiler_params=pltpu.CompilerParams(vmem_limit_bytes=LIMIT),
        name="forward",
    )(rows, cols, count, tiles, sketch)


def backward_kernel(parts, rows, cols, count, tiles, own, other, out, flat):
    s = pl.program_id(0)
    i = pl.program_id(1)
    core = lax.axis_index("core")
    depth, tb = tiles.shape

    @pl.when((s == 0) & (i == 0))
    def _():
        out[...] = jnp.zeros_like(out)
        for p in range(parts):
            flat[core, p] = own[p * depth : (p + 1) * depth, :].astype(BF16).T
            flat[1 - core, p] = other[p * depth : (p + 1) * depth, :].astype(BF16).T

    @pl.when(s < count[0])
    def _():
        prod = dot(flat[rows[s], i], tiles[...], ((1,), (0,)))
        half = tb // 2
        for q in range(2):
            out[2 * cols[s] + q] += prod[:, q * half : (q + 1) * half]


def backward(rows, cols, count, tiles, own, other):
    slots, tb, _ = tiles.shape
    width = own.shape[-1]
    parts = 2
    whole = pl.BlockSpec((tb, width), lambda s, i, *_: (0, 0))
    shape = (4, width, tb // 2)
    return pl.pallas_call(
        functools.partial(backward_kernel, parts),
        grid_spec=pltpu.PrefetchScalarGridSpec(
            num_scalar_prefetch=3,
            grid=(slots, parts),
            in_specs=[tile_spec(tb, parts), whole, whole],
            out_specs=pl.BlockSpec(shape, lambda s, i, *_: (0, 0, 0)),
            scratch_shapes=[pltpu.VMEM((2, parts, width, tb // parts), BF16)],
        ),
        out_shape=jax.ShapeDtypeStruct(shape, F32),
        compiler_params=pltpu.CompilerParams(vmem_limit_bytes=LIMIT),
        name="backward",
    )(rows, cols, count, tiles, own, other)


def block_pairs(n):
    return [(i, j) for i in range(n) for j in range(i, n)]


def gram_kernel(parts, zt, keep, send):
    core = lax.axis_index("core")
    narrow = parts.shape[1]
    zt[0:narrow, :] = parts[0] + parts[2]
    zt[narrow:, :] = parts[1] + parts[3]
    width = zt.shape[0]
    pairs = block_pairs(width // SIDE)
    half = len(pairs) // 2
    for i in range(width // SIDE):
        lhs = zt[i * SIDE : (i + 1) * SIDE, :]
        prod = dot(lhs, zt[i * SIDE :, :], ((1,), (1,)), HIGH)
        for n, (a, b) in enumerate(pairs):
            if a != i:
                continue
            block = prod[:, (b - i) * SIDE : (b - i + 1) * SIDE]

            @pl.when(core == n // half)
            def _():
                keep[n % half] = block

            @pl.when(core != n // half)
            def _():
                send[n % half] = block


def gram_of(parts):
    _, narrow, chunk = parts.shape
    width = 2 * narrow
    half = len(block_pairs(width // SIDE)) // 2
    blocks = jax.ShapeDtypeStruct((half, SIDE, SIDE), F32)
    return pl.pallas_call(
        gram_kernel,
        out_shape=[jax.ShapeDtypeStruct((width, chunk), F32), blocks, blocks],
        compiler_params=pltpu.CompilerParams(vmem_limit_bytes=LIMIT),
        name="gram",
    )(parts)


def eliminate(d, base):
    count = SUB // GROUP
    lanes = d.shape[1] // SIDE
    sub = lax.broadcasted_iota(jnp.int32, (GROUP, SIDE), 0)
    rows = [
        [d[base + GROUP * p : base + GROUP * (p + 1), SIDE * t : SIDE * (t + 1)] for t in range(lanes)]
        for p in range(count)
    ]
    for b in range(count):
        first = base + GROUP * b
        cols = [
            [jnp.broadcast_to(rows[p][0][:, first + m : first + m + 1], (GROUP, SIDE)) for p in range(b, count)]
            for m in range(GROUP)
        ]
        scale = jnp.zeros((GROUP, SIDE), F32)
        for m in range(GROUP):
            pivot = jnp.broadcast_to(cols[m][0][m : m + 1, :], (GROUP, SIDE))
            inv = lax.rsqrt(pivot)
            scale = jnp.where(sub == m, inv, scale)
            low = [c * inv for c in cols[m]]
            low[0] = jnp.where(sub > m, low[0], 0.0)
            for n in range(m + 1, GROUP):
                mult = jnp.broadcast_to(low[0][n : n + 1, :], (GROUP, SIDE))
                cols[n] = [c - l * mult for c, l in zip(cols[n], low)]
            for t in range(lanes):
                u = jnp.broadcast_to(rows[b][t][m : m + 1, :], (GROUP, SIDE)) * inv
                for p in range(b, count):
                    rows[p][t] = rows[p][t] - low[p - b] * u
        for t in range(lanes):
            rows[b][t] = rows[b][t] * scale
    for p in range(count):
        for t in range(lanes):
            d[base + GROUP * p : base + GROUP * (p + 1), SIDE * t : SIDE * (t + 1)] = rows[p][t]


def cholesky_kernel(scale, own, other, upper, inverse, d):
    core = lax.axis_index("core")
    width = upper.shape[0]
    nb = width // SIDE
    pairs = block_pairs(nb)
    half = len(pairs) // 2
    upper[...] = jnp.zeros_like(upper)
    inverse[...] = jnp.zeros_like(inverse)
    for n, (i, j) in enumerate(pairs):
        spot = (slice(i * SIDE, (i + 1) * SIDE), slice(j * SIDE, (j + 1) * SIDE))

        @pl.when(core == n // half)
        def _():
            upper[spot] = own[n % half] * scale

        @pl.when(core != n // half)
        def _():
            upper[spot] = other[n % half] * scale

    row = lax.broadcasted_iota(jnp.int32, (SIDE, SIDE), 0)
    col = lax.broadcasted_iota(jnp.int32, (SIDE, SIDE), 1)
    eye = (row == col).astype(F32)

    def step(k, carry):
        here = pl.ds(pl.multiple_of(k * SIDE, SIDE), SIDE)
        d[:, 0:SIDE] = upper[here, here]
        d[:, SIDE:] = eye
        for s in range(SIDE // SUB):
            base = s * SUB
            eliminate(d, base)
            if base + SUB < SIDE:
                panel = d[base : base + SUB, :]
                left = panel[:, base + SUB : SIDE]
                d[base + SUB :, :] -= dot(left, panel, ((0,), (0,)), HIGH)
        upper[here, here] = jnp.where(row <= col, d[:, 0:SIDE], 0.0)
        inverse[here, here] = jnp.where(row >= col, d[:, SIDE:], 0.0)

        for kk in range(nb):

            @pl.when(k == kk)
            def _():
                lo, hi = kk * SIDE, (kk + 1) * SIDE
                w = inverse[lo:hi, lo:hi]
                if hi < width:
                    upper[lo:hi, hi:] = dot(w, upper[lo:hi, hi:], ((1,), (0,)), HIGH)
                if lo > 0:
                    inverse[lo:hi, 0:lo] = dot(w, inverse[lo:hi, 0:lo], ((1,), (0,)), HIGH)
                if hi < width:
                    left = upper[lo:hi, hi:].T
                    prod = dot(left, upper[lo:hi, hi:], ((1,), (0,)), HIGH)
                    for i in range(kk + 1, nb):
                        r = slice(i * SIDE, (i + 1) * SIDE)
                        o = slice((i - kk - 1) * SIDE, (i - kk) * SIDE)
                        upper[r, i * SIDE :] -= prod[o, (i - kk - 1) * SIDE :]
                    inverse[hi:, 0:hi] -= dot(left, inverse[lo:hi, 0:hi], ((1,), (0,)), HIGH)

        return carry

    lax.fori_loop(0, nb, step, 0)


def cholesky(own, other, total_rows, width):
    square = jax.ShapeDtypeStruct((width, width), F32)
    return pl.pallas_call(
        functools.partial(cholesky_kernel, 1.0 / total_rows),
        out_shape=[square, square],
        scratch_shapes=[pltpu.VMEM((SIDE, 2 * SIDE), F32)],
        compiler_params=pltpu.CompilerParams(vmem_limit_bytes=LIMIT),
        name="cholesky",
    )(own, other)


def basis_kernel(sk, inverse, zt, out):
    out[...] = dot(inverse[...], zt[...], ((1,), (0,)), HIGH).T


def basis_of(inverse, zts, sk):
    width = inverse.shape[0]
    narrow = width // 2
    quarters, _, chunk = zts.shape
    return pl.pallas_call(
        basis_kernel,
        grid_spec=pltpu.PrefetchScalarGridSpec(
            num_scalar_prefetch=1,
            grid=(quarters,),
            in_specs=[
                pl.BlockSpec((narrow, width), lambda q, sk: (sk[0], 0)),
                pl.BlockSpec((None, width, chunk), lambda q, sk: (q, 0, 0)),
            ],
            out_specs=pl.BlockSpec((chunk, narrow), lambda q, sk: (q, 0)),
        ),
        out_shape=jax.ShapeDtypeStruct((quarters * chunk, narrow), F32),
        compiler_params=pltpu.CompilerParams(vmem_limit_bytes=LIMIT),
        name="basis",
    )(sk, inverse, zts)


def swap(x):
    return lax.ppermute(x, "core", [(0, 1), (1, 0)])


def exchange(x, axes):
    return lax.all_to_all(x, axes, 0, 0, tiled=True)


def spread(x, axes):
    n = lax.axis_size(axes)
    return exchange(jnp.broadcast_to(x[None], (n,) + x.shape), axes)


def on_device(tiles, tile_rows, tile_cols, tile_count, sketch):
    blocks = tiles[0, 0]
    rows = tile_rows[0, 0]
    cols = tile_cols[0, 0]
    count = tile_count[0]
    tb = blocks.shape[1]
    narrow = sketch.shape[1]
    width = narrow * lax.axis_size("sk")
    total_rows = sketch.shape[0] * lax.axis_size(("z", "y", "core"))

    keep, send = forward(rows, cols, count, blocks, sketch.reshape(-1, tb, narrow))
    half = keep + swap(send)
    plane = lax.axis_size(PLANE)
    pieces = exchange(half.reshape(plane, tb // plane, narrow), PLANE)
    piece = jnp.sum(pieces, axis=0) * 0.75
    own_y = spread(piece, PLANE).reshape(tb, narrow)
    other_y = swap(own_y)

    quarters = backward(rows, cols, count, blocks, own_y, other_y)
    zt, keep, send = gram_of(exchange(quarters, RING))
    zts = lax.all_gather(zt, RING, axis=0)

    half = keep + swap(send)
    sheet = lax.axis_size(SHEET)
    pieces = exchange(half.reshape(sheet, -1, SIDE), SHEET)
    piece = jnp.sum(pieces, axis=0)
    piece = jnp.sum(spread(piece, "z"), axis=0)
    own_g = spread(piece, SHEET).reshape(keep.shape)
    other_g = swap(own_g)

    upper, inverse = cholesky(own_g, other_g, total_rows, width)
    sk = lax.axis_index("sk").astype(jnp.int32).reshape(1)
    return basis_of(inverse, zts, sk), upper


def solution(mesh):
    fine = Mesh(mesh.devices.reshape(2, 8, 4, 2, 2), ("row", "z", "y", "core", "sk"))
    col = ("z", "y", "core")
    return jax.shard_map(
        on_device,
        mesh=fine,
        in_specs=(
            P("row", col, None, None, None),
            P("row", col, None),
            P("row", col, None),
            P("row", col),
            P(col, "sk"),
        ),
        out_specs=(P(col, "sk"), P()),
        check_vma=False,
    )
```

time: 767 us -> 225 us (0.29)
  waiting for transfers between devices: 515 us -> 8.56 us
  blocking collectives: 0 us -> 151 us
  other arithmetic: 126 us -> 0.3 us
  matrix products: 66.5 us -> 0 us
  Pallas kernels: 0 us -> 41.5 us
  local copies, waits for them, and re-layouts: 33.9 us -> 4.87 us
    psum x3 -> x0, waiting for transfers between devices: 452 us -> none  [the longest x1 192 us: on_device(): summed_y = lax.psum(partial_y, 'col')]
    all_to_all x0 -> x6, blocking collectives: none -> 151 us  [exchange(): return lax.all_to_all(x, axes, 0, 0, tiled=True)]
    another operation x16 -> x0, other arithmetic: 119 us -> none  [the longest x14 78.8 us: on_device(): lower = jnp.linalg.cholesky(gram)]
    all_gather x1, waiting for transfers between devices: 63 us -> 0.01 us  [on_device(): zts = lax.all_gather(zt, RING, axis=0)]
    dot_general x6 -> x0, matrix products: 53.3 us -> none  [the longest x2 18.4 us: slab_product(): return jnp.einsum('sg,sik->gik', weights, prod, precision=high)]
    pallas_call x0 -> x5, Pallas kernels: none -> 41.5 us  [the longest x1 21.1 us: cholesky(): pl.pallas_call(functools.partial(cholesky_kernel, 1.0 / total_rows), out_...]
    another operation x17 -> x0, local copies, waits for them, and re-layouts: 13.9 us -> none
    dot_general x4 -> x0, local copies, waits for them, and re-layouts: 13.5 us -> none  [the longest x2 10.5 us: slab_product(): prod = jnp.einsum(form, blocks, picked, preferred_element_type=jnp.float32)]
  transfers between devices with their start and end apart: 4 -> 5, of which waited for: 4 -> 4; matrix products, arithmetic and copies ran while one was open for 0% -> 0% of each run, Pallas kernels for 0% -> 10%
where the time goes in v1:
time: 225 us; the launch traced here: 222 us
  blocking collectives  151 us (67%)
  Pallas kernels  41.5 us (18%)
  between operations  14.8 us (7%)
  waiting for transfers between devices  8.56 us (4%)
  local copies, waits for them, and re-layouts  4.87 us (2%)
    all_to_all x6, blocking collectives, exchange(): return lax.all_to_all(x, axes, 0, 0, tiled=True)  151 us
    pallas_call x1, Pallas kernels, cholesky(): pl.pallas_call(functools.partial(cholesky_kernel, 1.0 / total_rows), out_...  21.1 us
    ppermute x4, waiting for transfers between devices, swap(): return lax.ppermute(x, 'core', [(0, 1), (1, 0)])  8.55 us
    pallas_call x1, Pallas kernels, basis_of(): pl.pallas_call(basis_kernel, grid_spec=pltpu.PrefetchScalarGridSpec(num_s...  5.64 us
    pallas_call x1, Pallas kernels, backward(): pl.pallas_call(functools.partial(backward_kernel, parts), grid_spec=pltpu...  5.08 us
    pallas_call x1, Pallas kernels, forward(): pl.pallas_call(functools.partial(forward_kernel, parts), grid_spec=pltpu....  4.97 us
    unnamed x12, local copies, waits for them, and re-layouts  4.72 us
    pallas_call x1, Pallas kernels, gram_of(): pl.pallas_call(gram_kernel, out_shape=[jax.ShapeDtypeStruct((width, chunk...  4.71 us
  transfers between devices with their start and end apart: 5, of which 4 were waited for; matrix products, arithmetic and copies ran while one was open for 0% of the time, Pallas kernels for 10%

profile of v1, /device:TPU:2, one launch (start us, length us, event | category | flops | bytes accessed | tf_op | source)
XLA Modules:
  0.0 221.7 jit_solution(7971039195729960090)
XLA Ops:
  7.2 0.0 all-gather.3.cloned.1.call-start
  7.9 0.0 copy-start.1
  7.9 1.2 copy-done.1
  9.1 0.0 copy-start.2
  9.1 0.7 copy-done.2
  9.7 0.0 copy-start.4
  9.7 0.7 copy-done.4
  10.4 5.0 %forward.1 = (f32[1024,256]{1,0:T(8,128)S(1)}, f32[1024,256]{1,0:T(8,128)S(1)}) custom-call(s32[4]{0:T(128)S(1)} %bitcast.19, s32[4]{0:T(128)S(1)} %bitcast.21, s32[1]{0:T(128)} %bitcast.11.count, bf16[4,1024,1024]{2,1,0:T(8,128)(2,1)} %bitcast.23, bf16[2,1024,256]{2,1,0:T(8,128)(2,1)S(1)} %bitcast.18), custom_call_target="tpu_custom_call" | custom-call | tf_op jit(solution)/shard_map/forward/pallas_call | solution.py:65
  15.4 0.1 collective-permute-start
  15.5 2.6 %collective-permute-done = f32[1024,256]{1,0:T(8,128)S(1)} collective-permute-done((f32[1024,256]{1,0:T(8,128)S(1)}, f32[1024,256]{1,0:T(8,128)S(1)}, u32[]{:S(2)}, u32[]{:S(2)}) %collective-permute-start) | collective-permute-done | bytes 1048608 | tf_op jit(solution)/shard_map/ppermute | solution.py:296
  18.1 0.1 add.6
  18.3 42.6 %all_to_all.30 = f32[32,32,256]{2,1,0:T(8,128)S(1)} all-to-all(f32[32,32,256]{2,1,0:T(8,128)S(1)} %bitcast.25), channel_id=1, replica_groups=mesh['row'=2,'z'=8,'y'=4,'core'=2,'sk'=2] {'z','y'}, dimensions={0} | all-to-all | bytes 2097152 | tf_op jit(solution)/shard_map/all_to_all | solution.py:300
  60.9 0.0 copy-start.3
  60.9 0.0 copy-start.5
  60.9 0.1 reduce_sum.27
  61.0 0.1 broadcast_in_dim.6
  61.1 32.8 %all_to_all.31 = f32[32,32,256]{2,1,0:T(8,128)S(1)} all-to-all(f32[32,32,256]{2,1,0:T(8,128)S(1)} %broadcast_in_dim.6), channel_id=1, replica_groups=mesh['row'=2,'z'=8,'y'=4,'core'=2,'sk'=2] {'z','y'}, dimensions={0} | all-to-all | bytes 2097152 | tf_op jit(solution)/shard_map/all_to_all | solution.py:300
  93.8 0.0 collective-permute-start.1
  93.8 2.7 %collective-permute-done.1.other = f32[1024,256]{1,0:T(8,128)S(1)} collective-permute-done((f32[1024,256]{1,0:T(8,128)S(1)}, f32[1024,256]{1,0:T(8,128)S(1)}, u32[]{:S(2)}, u32[]{:S(2)}) %collective-permute-start.1) | collective-permute-done | bytes 1048608 | tf_op jit(solution)/shard_map/ppermute | solution.py:296
  96.5 0.0 copy-done.3
  96.5 0.0 copy-done.5
  96.5 5.1 %backward.1 = f32[4,256,512]{2,1,0:T(8,128)S(1)} custom-call(s32[4]{0:T(128)S(1)} %bitcast.20, s32[4]{0:T(128)S(1)} %bitcast.22, s32[1]{0:T(128)} %bitcast.12.count, bf16[4,1024,1024]{2,1,0:T(8,128)(2,1)} %bitcast.24, f32[1024,256]{1,0:T(8,128)S(1)} %bitcast.14, f32[1024,256]{1,0:T(8,128)S(1)} %collective-permute-done.1.other), custom_call_target="tpu_custom_call" | custom-call | tf_op jit(solution)/shard_map/backward/pallas_call | solution.py:106
  101.6 30.2 %all_to_all.32.parts = f32[4,256,512]{2,1,0:T(8,128)S(1)} all-to-all(f32[4,256,512]{2,1,0:T(8,128)S(1)} %backward.1), channel_id=1, replica_groups=mesh['row'=2,'z'=8,'y'=4,'core'=2,'sk'=2] {'row','sk'}, dimensions={0} | all-to-all | bytes 4194304 | tf_op jit(solution)/shard_map/all_to_all | solution.py:300
  131.8 4.7 %gram.1 = (f32[512,512]{1,0:T(8,128)}, f32[5,128,128]{2,1,0:T(8,128)S(1)}, f32[5,128,128]{2,1,0:T(8,128)S(1)}) custom-call(f32[4,256,512]{2,1,0:T(8,128)S(1)} %all_to_all.32.parts), custom_call_target="tpu_custom_call" | custom-call | tf_op jit(solution)/shard_map/gram/pallas_call | solution.py:155
  136.5 0.0 all-gather.3.cloned.1.call-update
  136.5 0.1 collective-permute-start.2
  136.6 1.6 collective-permute-done.2
  138.2 0.1 add.7
  138.3 16.8 %all_to_all.33 = f32[16,40,128]{2,1,0:T(8,128)S(1)} all-to-all(f32[16,40,128]{2,1,0:T(8,128)S(1)} %bitcast.26), channel_id=1, replica_groups=mesh['row'=2,'z'=8,'y'=4,'core'=2,'sk'=2] {'row','y','sk'}, dimensions={0} | all-to-all | bytes 655360 | tf_op jit(solution)/shard_map/all_to_all | solution.py:300
  155.1 13.0 %all_to_all.34 = f32[8,40,128]{2,1,0:T(8,128)S(1)} all-to-all(f32[8,40,128]{2,1,0:T(8,128)S(1)} %broadcast_in_dim.7), channel_id=1, replica_groups=mesh['row'=2,'z'=8,'y'=4,'core'=2,'sk'=2] {'z'}, dimensions={0} | all-to-all | bytes 327680 | tf_op jit(solution)/shard_map/all_to_all | solution.py:300
  168.2 16.0 %all_to_all.35 = f32[16,40,128]{2,1,0:T(8,128)S(1)} all-to-all(f32[16,40,128]{2,1,0:T(8,128)S(1)} %broadcast_in_dim.8), channel_id=1, replica_groups=mesh['row'=2,'z'=8,'y'=4,'core'=2,'sk'=2] {'row','y','sk'}, dimensions={0} | all-to-all | bytes 655360 | tf_op jit(solution)/shard_map/all_to_all | solution.py:300
  184.2 0.0 collective-permute-start.3
  184.2 1.6 collective-permute-done.3.other
  185.8 21.1 %cholesky.1 = (f32[512,512]{1,0:T(8,128)}, f32[512,512]{1,0:T(8,128)S(1)}) custom-call(f32[5,128,128]{2,1,0:T(8,128)S(1)} %bitcast.17, f32[5,128,128]{2,1,0:T(8,128)S(1)} %collective-permute-done.3.other), custom_call_target="tpu_custom_call" | custom-call | tf_op jit(solution)/shard_map/cholesky/pallas_call | solution.py:261
  207.0 0.0 all-gather.3.cloned.1.call-done
  207.0 0.0 copy-start
  207.0 2.2 copy-done
  209.2 5.6 %basis.1 = f32[2048,256]{1,0:T(8,128)} custom-call(s32[1]{0:T(128)} %bitcast.sk, f32[512,512]{1,0:T(8,128)S(1)} %get-tuple-element.13.inverse, f32[4,512,512]{2,1,0:T(8,128)S(1)} %bitcast.15), custom_call_target="tpu_custom_call" | custom-call | tf_op jit(solution)/shard_map/basis/pallas_call | solution.py:278
  (5 shorter events, 0.1 us)
Async XLA Ops:
  7.2 199.8 %all-gather.3.cloned.1.call-start = ((), (), s32[]{:S(2)}) async-start(), calls=%async_computation.6 | async-start | bytes 5242880 | tf_op jit(solution)/shard_map/all_gather | solution.py:328
  7.9 1.2 copy-start.1
  9.1 0.7 copy-start.2
  9.7 0.7 copy-start.4
  15.4 2.7 %collective-permute-start = (f32[1024,256]{1,0:T(8,128)S(1)}, f32[1024,256]{1,0:T(8,128)S(1)}, u32[]{:S(2)}, u32[]{:S(2)}) collective-permute-start(f32[1024,256]{1,0:T(8,128)S(1)} %get-tuple-element.10), channel_id=1, source_target_pairs={{0,2},{2,0},{1,3},{3,1},{4,6},{6,4},{5,7},{7,5},{8,10},{10,8},{9,1... | collective-permute-start | bytes 3145736 | tf_op jit(solution)/shard_map/ppermute | solution.py:296
  60.9 35.6 %copy-start.3 = (s32[1,1,4]{2,1,0:T(1,128)S(1)}, s32[1,1,4]{2,1,0:T(1,128)}, u32[]{:S(2)}) copy-start(s32[1,1,4]{2,1,0:T(1,128)} %param.6) | copy-start | bytes 52
  60.9 35.6 %copy-start.5 = (s32[1,1,4]{2,1,0:T(1,128)S(1)}, s32[1,1,4]{2,1,0:T(1,128)}, u32[]{:S(2)}) copy-start(s32[1,1,4]{2,1,0:T(1,128)} %param.7) | copy-start | bytes 52
  93.8 2.7 %collective-permute-start.1 = (f32[1024,256]{1,0:T(8,128)S(1)}, f32[1024,256]{1,0:T(8,128)S(1)}, u32[]{:S(2)}, u32[]{:S(2)}) collective-permute-start(f32[1024,256]{1,0:T(8,128)S(1)} %bitcast.13), channel_id=1, source_target_pairs={{0,2},{2,0},{1,3},{3,1},{4,6},{6,4},{5,7},{7,5},{8,10},{10,8},{9,1... | collective-permute-start | bytes 3145736 | tf_op jit(solution)/shard_map/ppermute | solution.py:296
  136.5 1.7 collective-permute-start.2
  184.2 1.6 collective-permute-start.3
  207.0 2.2 copy-start
Sparse Core Ops, SparseCore 0:
  136.6 53.1 all-gather.2

commit v2 on v1

v2 whole, which is shorter than its diff:
```python
import functools

import jax
import jax.numpy as jnp
from jax import lax
from jax.experimental import pallas as pl
from jax.experimental.pallas import tpu as pltpu
from jax.sharding import Mesh, PartitionSpec as P

HIGH = lax.Precision.HIGHEST
F32 = jnp.float32
BF16 = jnp.bfloat16
RING = ("row", "sk")
SHEET = ("row", "y", "sk")
LIMIT = 48 * 1024 * 1024
SIDE = 128
GROUP = 8
SUB = 32


def dot(a, b, dims, precision=None):
    return lax.dot_general(a, b, (dims, ((), ())), precision=precision, preferred_element_type=F32)


PARTS = 4


def fetch(tiles, held, sems):
    slots, tb, _ = tiles.shape
    depth = tb // PARTS
    copies = [
        [
            pltpu.make_async_copy(
                tiles.at[s, pl.ds(p * depth, depth)], held.at[s, pl.ds(p * depth, depth)], sems.at[s, p]
            )
            for p in range(PARTS)
        ]
        for s in range(slots)
    ]
    for slot in copies[:2]:
        for copy in slot:
            copy.start()
    return copies


def await_tile(copies, s):
    for copy in copies[s]:
        copy.wait()
    for copy in copies[s + 2] if s + 2 < len(copies) else []:
        copy.start()


def forward_kernel(rows, cols, count, tiles, sketch, keep, send, held, sems):
    copies = fetch(tiles, held, sems)
    core = lax.axis_index("core")
    y = lax.axis_index("y")
    slots, tb, _ = held.shape
    depth = tb // PARTS
    keep[...] = jnp.zeros_like(keep)
    send[...] = jnp.zeros_like(send)
    for s in range(slots):
        await_tile(copies, s)

        def add(out):
            prod = dot(held[s], sketch[cols[s]], ((1,), (0,)))
            for p in range(PARTS):
                away = lax.rem(p - y + PARTS, PARTS)
                for h in range(2):
                    out[away, h] += prod[p * depth : (p + 1) * depth, h * SIDE : (h + 1) * SIDE]

        @pl.when((s < count[0]) & (rows[s] == core))
        def _():
            add(keep)

        @pl.when((s < count[0]) & (rows[s] != core))
        def _():
            add(send)


SMEM = pl.BlockSpec(memory_space=pltpu.SMEM)
VMEM = pl.BlockSpec(memory_space=pltpu.VMEM)
ANY = pl.BlockSpec(memory_space=pl.ANY)


def forward(rows, cols, count, tiles, sketch):
    slots, tb, _ = tiles.shape
    width = sketch.shape[-1]
    half = jax.ShapeDtypeStruct((PARTS, width // SIDE, tb // PARTS, SIDE), F32)
    return pl.pallas_call(
        forward_kernel,
        in_specs=[SMEM, SMEM, SMEM, ANY, VMEM],
        out_specs=[VMEM, VMEM],
        out_shape=[half, half],
        scratch_shapes=[pltpu.VMEM(tiles.shape, BF16), pltpu.SemaphoreType.DMA((slots, PARTS))],
        compiler_params=pltpu.CompilerParams(vmem_limit_bytes=LIMIT),
        name="forward",
    )(rows, cols, count, tiles, sketch)


def backward_kernel(rows, cols, count, tiles, *rest):
    own, other = rest[:PARTS], rest[PARTS : 2 * PARTS]
    outs = rest[2 * PARTS : 2 * PARTS + 4]
    out, flat, held, sems = rest[2 * PARTS + 4 :]
    copies = fetch(tiles, held, sems)
    core = lax.axis_index("core")
    y = lax.axis_index("y")
    here = 2 * lax.axis_index("row") + lax.axis_index("sk")
    slots, tb, _ = held.shape
    depth = tb // PARTS
    out[...] = jnp.zeros_like(out)
    for block, pieces in ((core, own), (1 - core, other)):
        for away, piece in enumerate(pieces):
            part = lax.rem(y - away + PARTS, PARTS)
            here_part = pl.ds(pl.multiple_of(part * depth, depth), depth)
            for h in range(piece.shape[0]):
                flat[block, h * SIDE : (h + 1) * SIDE, here_part] = piece[h].astype(BF16).T
    for s in range(slots):
        await_tile(copies, s)

        @pl.when(s < count[0])
        def _():
            prod = dot(flat[rows[s]], held[s], ((1,), (0,)))
            for q in range(2):
                for n in range(tb // 2 // SIDE):
                    at = q * (tb // 2) + n * SIDE
                    out[2 * cols[s] + q, n] += prod[:, at : at + SIDE]

    for n in range(4):
        outs[n][...] = out[here ^ n]


def backward(rows, cols, count, tiles, own, other):
    slots, tb, _ = tiles.shape
    width = own[0].shape[0] * SIDE
    quarter = (tb // 2 // SIDE, width, SIDE)
    return pl.pallas_call(
        backward_kernel,
        in_specs=[SMEM, SMEM, SMEM, ANY] + [VMEM] * (2 * PARTS),
        out_specs=[VMEM] * 4,
        out_shape=[jax.ShapeDtypeStruct(quarter, F32)] * 4,
        scratch_shapes=[
            pltpu.VMEM((4,) + quarter, F32),
            pltpu.VMEM((2, width, tb), BF16),
            pltpu.VMEM(tiles.shape, BF16),
            pltpu.SemaphoreType.DMA((slots, PARTS)),
        ],
        compiler_params=pltpu.CompilerParams(vmem_limit_bytes=LIMIT),
        name="backward",
    )(rows, cols, count, tiles, *own, *other)


def block_pairs(n):
    return [(i, j) for i in range(n) for j in range(i, n)]


def gram_kernel(*refs):
    zt, keep, send = refs[-3:]
    core = lax.axis_index("core")
    sk = lax.axis_index("sk")
    parts = refs[0:4]
    chunks, narrow, _ = refs[0].shape
    for far in range(2):
        rows = pl.ds(pl.multiple_of((sk ^ far) * narrow, narrow), narrow)
        for n in range(chunks):
            zt[rows, n * SIDE : (n + 1) * SIDE] = parts[far][n] + parts[far + 2][n]
    width = zt.shape[0]
    pairs = block_pairs(width // SIDE)
    half = len(pairs) // 2
    for i in range(width // SIDE):
        lhs = zt[i * SIDE : (i + 1) * SIDE, :]
        prod = dot(lhs, zt[i * SIDE :, :], ((1,), (1,)), HIGH)
        for n, (a, b) in enumerate(pairs):
            if a != i:
                continue
            block = prod[:, (b - i) * SIDE : (b - i + 1) * SIDE]

            @pl.when(core == n // half)
            def _():
                keep[n % half] = block

            @pl.when(core != n // half)
            def _():
                send[n % half] = block


def gram_of(parts):
    chunks, deep, _ = parts[0].shape
    width = 2 * deep
    half = len(block_pairs(width // SIDE)) // 2
    blocks = jax.ShapeDtypeStruct((half, SIDE, SIDE), F32)
    return pl.pallas_call(
        gram_kernel,
        in_specs=[VMEM] * len(parts),
        out_specs=[VMEM] * 3,
        out_shape=[jax.ShapeDtypeStruct((width, chunks * SIDE), F32), blocks, blocks],
        compiler_params=pltpu.CompilerParams(vmem_limit_bytes=LIMIT),
        name="gram",
    )(*parts)


def spread_rows(x, n):
    return jnp.broadcast_to(x[n : n + 1, :], (GROUP, SIDE))


def spread_lanes(x, n):
    return jnp.broadcast_to(x[:, n : n + 1], (GROUP, SIDE))


def eliminate(d, base):
    count = SUB // GROUP
    lanes = d.shape[1] // SIDE
    sub = lax.broadcasted_iota(jnp.int32, (GROUP, SIDE), 0)
    rows = [
        [d[base + GROUP * p : base + GROUP * (p + 1), SIDE * t : SIDE * (t + 1)] for t in range(lanes)]
        for p in range(count)
    ]

    def columns(b):
        first = base + GROUP * b
        return [[spread_lanes(rows[p][0], first + m) for p in range(b, count)] for m in range(GROUP)]

    cols = columns(0)
    for b in range(count):
        ahead = columns(b + 1) if b + 1 < count else []
        scale = jnp.zeros((GROUP, SIDE), F32)
        for m in range(GROUP):
            col = cols[m]
            inv = lax.rsqrt(spread_rows(col[0], m))
            inv2 = inv * inv
            for n in range(m + 1, GROUP):
                mult = spread_rows(col[0], n)
                cols[n] = [c - (l * mult) * inv2 for c, l in zip(cols[n], col)]
            scale = jnp.where(sub == m, inv, scale)
            low = [jnp.where(sub > m, col[0], 0.0) * inv2] + [l * inv2 for l in col[1:]]
            for n in range(len(ahead)):
                mult = spread_rows(col[1], n)
                ahead[n] = [c - l * mult for c, l in zip(ahead[n], low[1:])]
            for t in range(lanes):
                u = spread_rows(rows[b][t], m)
                for p in range(b, count):
                    rows[p][t] = rows[p][t] - low[p - b] * u
        for t in range(lanes):
            rows[b][t] = rows[b][t] * scale
        cols = ahead
    for p in range(count):
        for t in range(lanes):
            d[base + GROUP * p : base + GROUP * (p + 1), SIDE * t : SIDE * (t + 1)] = rows[p][t]


def cholesky_kernel(scale, own, other, upper, inverse, d):
    core = lax.axis_index("core")
    width = upper.shape[0]
    nb = width // SIDE
    pairs = block_pairs(nb)
    half = len(pairs) // 2
    upper[...] = jnp.zeros_like(upper)
    inverse[...] = jnp.zeros_like(inverse)
    for n, (i, j) in enumerate(pairs):
        spot = (slice(i * SIDE, (i + 1) * SIDE), slice(j * SIDE, (j + 1) * SIDE))

        @pl.when(core == n // half)
        def _():
            upper[spot] = own[n % half] * scale

        @pl.when(core != n // half)
        def _():
            upper[spot] = other[n % half] * scale

    row = lax.broadcasted_iota(jnp.int32, (SIDE, SIDE), 0)
    col = lax.broadcasted_iota(jnp.int32, (SIDE, SIDE), 1)
    eye = (row == col).astype(F32)

    def step(k, carry):
        here = pl.ds(pl.multiple_of(k * SIDE, SIDE), SIDE)
        d[:, 0:SIDE] = upper[here, here]
        d[:, SIDE:] = eye
        for s in range(SIDE // SUB):
            base = s * SUB
            eliminate(d, base)
            if base + SUB < SIDE:
                panel = d[base : base + SUB, :]
                left = panel[:, base + SUB : SIDE]
                d[base + SUB :, :] -= dot(left, panel, ((0,), (0,)), HIGH)
        upper[here, here] = jnp.where(row <= col, d[:, 0:SIDE], 0.0)
        inverse[here, here] = jnp.where(row >= col, d[:, SIDE:], 0.0)

        for kk in range(nb):

            @pl.when(k == kk)
            def _():
                lo, hi = kk * SIDE, (kk + 1) * SIDE
                w = inverse[lo:hi, lo:hi]
                if hi < width:
                    upper[lo:hi, hi:] = dot(w, upper[lo:hi, hi:], ((1,), (0,)), HIGH)
                if lo > 0:
                    inverse[lo:hi, 0:lo] = dot(w, inverse[lo:hi, 0:lo], ((1,), (0,)), HIGH)
                if hi < width:
                    left = upper[lo:hi, hi:].T
                    prod = dot(left, upper[lo:hi, hi:], ((1,), (0,)), HIGH)
                    for i in range(kk + 1, nb):
                        r = slice(i * SIDE, (i + 1) * SIDE)
                        o = slice((i - kk - 1) * SIDE, (i - kk) * SIDE)
                        upper[r, i * SIDE :] -= prod[o, (i - kk - 1) * SIDE :]
                    inverse[hi:, 0:hi] -= dot(left, inverse[lo:hi, 0:hi], ((1,), (0,)), HIGH)

        return carry

    lax.fori_loop(0, nb, step, 0)


def cholesky(own, other, total_rows, width):
    square = jax.ShapeDtypeStruct((width, width), F32)
    return pl.pallas_call(
        functools.partial(cholesky_kernel, 1.0 / total_rows),
        out_shape=[square, square],
        scratch_shapes=[pltpu.VMEM((SIDE, 2 * SIDE), F32)],
        compiler_params=pltpu.CompilerParams(vmem_limit_bytes=LIMIT),
        name="cholesky",
    )(own, other)


def split(x):
    high = x.astype(BF16)
    return high, (x - high.astype(F32)).astype(BF16)


def basis_kernel(inverse, quarters, out, held, done, load, store):
    chunk, narrow = done.shape[1:]
    loads = [pltpu.make_async_copy(quarters.at[n], held.at[n], load.at[n]) for n in range(4)]
    for copy in loads:
        copy.start()
    w = inverse[pl.ds(pl.multiple_of(lax.axis_index("sk") * narrow, narrow), narrow), :]
    w_high, w_low = split(w)
    stores = []
    for n in range(4):
        loads[n].wait()
        high, low = split(held[n])
        form = ((1,), (0,))
        done[n] = (dot(w_high, high, form) + (dot(w_high, low, form) + dot(w_low, high, form))).T
        stores.append(pltpu.make_async_copy(done.at[n], out.at[pl.ds(n * chunk, chunk), :], store.at[n]))
        stores[n].start()
    for copy in stores:
        copy.wait()


def basis_of(inverse, quarters):
    width = inverse.shape[0]
    narrow = width // 2
    chunk = quarters.shape[2]
    return pl.pallas_call(
        basis_kernel,
        in_specs=[VMEM, ANY],
        out_specs=ANY,
        out_shape=jax.ShapeDtypeStruct((4 * chunk, narrow), F32),
        scratch_shapes=[
            pltpu.VMEM((4, width, chunk), F32),
            pltpu.VMEM((4, chunk, narrow), F32),
            pltpu.SemaphoreType.DMA((4,)),
            pltpu.SemaphoreType.DMA((4,)),
        ],
        compiler_params=pltpu.CompilerParams(vmem_limit_bytes=LIMIT),
        name="basis",
    )(inverse, quarters)


def swap(x):
    return lax.ppermute(x, "core", [(0, 1), (1, 0)])


def shift(x, axes, n):
    size = lax.axis_size(axes)
    return lax.ppermute(x, axes, [(i, (i + n) % size) for i in range(size)])


def across(x, n):
    return lax.ppermute(x, RING, [(i, i ^ n) for i in range(4)])


def exchange(x, axes):
    return lax.all_to_all(x, axes, 0, 0, tiled=True)


def spread(x, axes):
    n = lax.axis_size(axes)
    return exchange(jnp.broadcast_to(x[None], (n,) + x.shape), axes)


def on_device(tiles, tile_rows, tile_cols, tile_count, sketch):
    blocks = tiles[0, 0]
    rows = tile_rows[0, 0]
    cols = tile_cols[0, 0]
    count = tile_count[0]
    tb = blocks.shape[1]
    narrow = sketch.shape[1]
    width = narrow * lax.axis_size("sk")
    total_rows = sketch.shape[0] * lax.axis_size(("z", "y", "core"))

    keep, send = forward(rows, cols, count, blocks, sketch.reshape(-1, tb, narrow))
    received = swap(send)
    pieces = [keep[n] + received[n] for n in range(PARTS)]
    for n in (1, 3, 2):
        pieces[n] = shift(pieces[n], "y", n)
    part = pieces[0] + pieces[1] + pieces[3] + pieces[2]
    deep = lax.axis_size("z")
    pieces = exchange(part.reshape(deep, -1, SIDE), "z")
    piece = jnp.sum(pieces, axis=0) * 0.75
    part = spread(piece, "z").reshape(part.shape)
    own = [part] + [shift(part, "y", n) for n in range(1, PARTS)]
    other = [swap(p) for p in own]
    pieces = backward(rows, cols, count, blocks, own, other)
    moved = [pieces[0]] + [across(pieces[n], n) for n in range(1, 4)]
    zt, keep, send = gram_of(moved)
    quarters = lax.all_gather(zt, RING, axis=0)

    half = keep + swap(send)
    sheet = lax.axis_size(SHEET)
    pieces = exchange(half.reshape(sheet, -1, SIDE), SHEET)
    piece = jnp.sum(pieces, axis=0)
    piece = jnp.sum(spread(piece, "z"), axis=0)
    own_g = spread(piece, SHEET).reshape(keep.shape)
    other_g = swap(own_g)

    upper, inverse = cholesky(own_g, other_g, total_rows, width)
    return basis_of(inverse, quarters), upper


def solution(mesh):
    fine = Mesh(mesh.devices.reshape(2, 8, 4, 2, 2), ("row", "z", "y", "core", "sk"))
    col = ("z", "y", "core")
    return jax.shard_map(
        on_device,
        mesh=fine,
        in_specs=(
            P("row", col, None, None, None),
            P("row", col, None),
            P("row", col, None),
            P("row", col),
            P(col, "sk"),
        ),
        out_specs=(P(col, "sk"), P()),
        check_vma=False,
    )
```

time: 225 us -> 203 us (0.902)
  blocking collectives: 151 us -> 76.5 us
  waiting for transfers between devices: 8.56 us -> 53.4 us
  starting transfers between devices: 0.23 us -> 14 us
  Pallas kernels: 41.5 us -> 35.9 us
    all_to_all x6 -> x5, blocking collectives: 151 us -> 76.5 us  [exchange(): return lax.all_to_all(x, axes, 0, 0, tiled=True)]
    ppermute x0 -> x9, waiting for transfers between devices: none -> 45.9 us  [the longest x3 24.1 us: across(): return lax.ppermute(x, RING, [(i, i ^ n) for i in range(4)])]
    ppermute x0 -> x9, starting transfers between devices: none -> 13.8 us  [the longest x6 10.2 us: shift(): return lax.ppermute(x, axes, [(i, (i + n) % size) for i in range(size)])]
    pallas_call x1, Pallas kernels: 21.1 us -> 17.5 us  [cholesky(): pl.pallas_call(functools.partial(cholesky_kernel, 1.0 / total_rows), out_...]
    ppermute x4 -> x7, waiting for transfers between devices: 8.55 us -> 7.41 us  [swap(): return lax.ppermute(x, 'core', [(0, 1), (1, 0)])]
  transfers between devices with their start and end apart: 5 -> 17, of which waited for: 4 -> 12; matrix products, arithmetic and copies ran while one was open for 0% -> 0% of each run, Pallas kernels for 10% -> 9%
where the time goes in v2:
time: 203 us; the launch traced here: 200 us
  blocking collectives  76.5 us (38%)
  waiting for transfers between devices  53.4 us (26%)
  Pallas kernels  35.9 us (18%)
  between operations  14.8 us (7%)
  starting transfers between devices  14 us (7%)
  local copies, waits for them, and re-layouts  4.78 us (2%)
    all_to_all x5, blocking collectives, exchange(): return lax.all_to_all(x, axes, 0, 0, tiled=True)  76.5 us
    ppermute x3, waiting for transfers between devices, across(): return lax.ppermute(x, RING, [(i, i ^ n) for i in range(4)])  24.1 us
    ppermute x6, waiting for transfers between devices, shift(): return lax.ppermute(x, axes, [(i, (i + n) % size) for i in range(size)])  21.9 us
    pallas_call x1, Pallas kernels, cholesky(): pl.pallas_call(functools.partial(cholesky_kernel, 1.0 / total_rows), out_...  17.5 us
    ppermute x6, starting transfers between devices, shift(): return lax.ppermute(x, axes, [(i, (i + n) % size) for i in range(size)])  10.2 us
    ppermute x7, waiting for transfers between devices, swap(): return lax.ppermute(x, 'core', [(0, 1), (1, 0)])  7.41 us
    pallas_call x1, Pallas kernels, gram_of(): pl.pallas_call(gram_kernel, in_specs=[VMEM] * len(parts), out_specs=[VMEM...  4.86 us
    pallas_call x1, Pallas kernels, backward(): pl.pallas_call(backward_kernel, in_specs=[SMEM, SMEM, SMEM, ANY] + [VMEM]...  4.83 us
  transfers between devices with their start and end apart: 17, of which 12 were waited for; matrix products, arithmetic and copies ran while one was open for 0% of the time, Pallas kernels for 9%

profile of v2, /device:TPU:2, one launch (start us, length us, event | category | flops | bytes accessed | tf_op | source)
XLA Modules:
  0.0 199.6 jit_solution(4651488141746508665)
XLA Ops:
  7.2 0.0 all-gather.3.cloned.1.call-start
  7.9 0.0 copy-start.1
  7.9 1.2 copy-done.1
  9.1 0.0 copy-start.2
  9.1 0.7 copy-done.2
  9.7 0.0 copy-start.4
  9.7 0.7 copy-done.4
  10.4 4.6 %forward.1 = (f32[4,2,256,128]{3,2,1,0:T(8,128)S(1)}, f32[4,2,256,128]{3,2,1,0:T(8,128)S(1)}) custom-call(s32[4]{0:T(128)S(1)} %bitcast.35, s32[4]{0:T(128)S(1)} %bitcast.37, s32[1]{0:T(128)} %bitcast.24.count, bf16[4,1024,1024]{2,1,0:T(8,128)(2,1)} %bitcast.39, bf16[2,1024,256]{2,1,0:T(8,128)(2,1)S(1)} %bitcast.29), custom_call_target="tpu_custom_call" | custom-call | tf_op jit(solution)/shard_map/forward/pallas_call | solution.py:89
  15.0 0.0 copy-start.3
  15.0 0.0 copy-start.5
  15.0 0.1 collective-permute-start
  15.1 2.6 %collective-permute-done = f32[4,2,256,128]{3,2,1,0:T(8,128)S(1)} collective-permute-done((f32[4,2,256,128]{3,2,1,0:T(8,128)S(1)}, f32[4,2,256,128]{3,2,1,0:T(8,128)S(1)}, u32[]{:S(2)}, u32[]{:S(2)}) %collective-permute-start) | collective-permute-done | bytes 1048608 | tf_op jit(solution)/shard_map/ppermute | solution.py:367
  17.8 0.1 fusion.2
  17.9 1.9 collective-permute-start.1
  19.7 2.9 %collective-permute-start.3 = (f32[2,256,128]{2,1,0:T(8,128)S(1)}, f32[2,256,128]{2,1,0:T(8,128)S(1)}, u32[]{:S(2)}, u32[]{:S(2)}) collective-permute-start(f32[2,256,128]{2,1,0:T(8,128)S(1)} %get-tuple-element.25), channel_id=1, source_target_pairs={{0,8},{4,12},{8,0},{12,4},{1,9},{5,13},{9,1},{13,5},{2,10},{6,14},... | collective-permute-start | bytes 786440 | tf_op jit(solution)/shard_map/ppermute | solution.py:372
  22.6 1.2 collective-permute-start.2
  23.8 4.2 %collective-permute-done.1 = f32[2,256,128]{2,1,0:T(8,128)S(1)} collective-permute-done((f32[2,256,128]{2,1,0:T(8,128)S(1)}, f32[2,256,128]{2,1,0:T(8,128)S(1)}, u32[]{:S(2)}, u32[]{:S(2)}) %collective-permute-start.1) | collective-permute-done | bytes 262176 | tf_op jit(solution)/shard_map/ppermute | solution.py:372
  28.0 6.8 %collective-permute-done.3 = f32[2,256,128]{2,1,0:T(8,128)S(1)} collective-permute-done((f32[2,256,128]{2,1,0:T(8,128)S(1)}, f32[2,256,128]{2,1,0:T(8,128)S(1)}, u32[]{:S(2)}, u32[]{:S(2)}) %collective-permute-start.3) | collective-permute-done | bytes 262176 | tf_op jit(solution)/shard_map/ppermute | solution.py:372
  34.8 0.0 collective-permute-done.2
  34.8 0.1 fusion.6
  34.9 19.5 %all_to_all.25 = f32[8,64,128]{2,1,0:T(8,128)S(1)} all-to-all(f32[8,64,128]{2,1,0:T(8,128)S(1)} %bitcast.42), channel_id=1, replica_groups=mesh['row'=2,'z'=8,'y'=4,'core'=2,'sk'=2] {'z'}, dimensions={0} | all-to-all | bytes 524288 | tf_op jit(solution)/shard_map/all_to_all | solution.py:380
  54.4 12.9 %all_to_all.26 = f32[8,64,128]{2,1,0:T(8,128)S(1)} all-to-all(f32[8,64,128]{2,1,0:T(8,128)S(1)} %broadcast_in_dim.6), channel_id=1, replica_groups=mesh['row'=2,'z'=8,'y'=4,'core'=2,'sk'=2] {'z'}, dimensions={0} | all-to-all | bytes 524288 | tf_op jit(solution)/shard_map/all_to_all | solution.py:380
  67.3 3.4 %collective-permute-start.6 = (f32[2,256,128]{2,1,0:T(8,128)S(1)}, f32[2,256,128]{2,1,0:T(8,128)S(1)}, u32[]{:S(2)}, u32[]{:S(2)}) collective-permute-start(f32[2,256,128]{2,1,0:T(8,128)S(1)} %bitcast.30), channel_id=1, source_target_pairs={{0,12},{4,0},{8,4},{12,8},{1,13},{5,1},{9,5},{13,9},{2,14},{6,2},{... | collective-permute-start | bytes 786440 | tf_op jit(solution)/shard_map/ppermute | solution.py:372
  70.7 0.3 collective-permute-start.5
  71.0 0.5 collective-permute-start.4
  71.5 0.0 collective-permute-start.7
  71.5 7.5 %collective-permute-done.6.rest_3_ = f32[2,256,128]{2,1,0:T(8,128)S(1)} collective-permute-done((f32[2,256,128]{2,1,0:T(8,128)S(1)}, f32[2,256,128]{2,1,0:T(8,128)S(1)}, u32[]{:S(2)}, u32[]{:S(2)}) %collective-permute-start.6) | collective-permute-done | bytes 262176 | tf_op jit(solution)/shard_map/ppermute | solution.py:372
  79.0 0.0 collective-permute-start.10
  79.0 1.0 collective-permute-done.5.rest_2_
  80.0 0.0 collective-permute-start.9
  80.0 2.4 %collective-permute-done.4.rest_1_ = f32[2,256,128]{2,1,0:T(8,128)S(1)} collective-permute-done((f32[2,256,128]{2,1,0:T(8,128)S(1)}, f32[2,256,128]{2,1,0:T(8,128)S(1)}, u32[]{:S(2)}, u32[]{:S(2)}) %collective-permute-start.4) | collective-permute-done | bytes 262176 | tf_op jit(solution)/shard_map/ppermute | solution.py:372
  82.4 0.0 collective-permute-start.8
  82.4 0.0 collective-permute-done.7.rest_4_
  82.4 0.0 collective-permute-done.10.rest_7_
  82.4 0.0 collective-permute-done.9.rest_6_
  82.4 1.5 collective-permute-done.8.rest_5_
  83.9 0.0 copy-done.3
  83.9 0.0 copy-done.5
  83.9 4.8 %backward.1 = (f32[4,256,128]{2,1,0:T(8,128)S(1)}, f32[4,256,128]{2,1,0:T(8,128)S(1)}, f32[4,256,128]{2,1,0:T(8,128)S(1)}, f32[4,256,128]{2,1,0:T(8,128)S(1)}) custom-call(s32[4]{0:T(128)S(1)} %bitcast.36, s32[4]{0:T(128)S(1)} %bitcast.38, s32[1]{0:T(128)} %bitcast.25.count, bf16[4,1024,1024]{2,1,0:T(8,128)(2,1)} %bitcast.40, f32[2,256,128]{2,1,0:T(8,128)S(1)} %bitcast.34, ...), custom_call_target="tpu_custom_call" | custom-call | tf_op jit(solution)/shard_map/backward/pallas_call | solution.py:136
  88.8 0.6 collective-permute-start.11
  89.4 2.4 %collective-permute-start.12 = (f32[4,256,128]{2,1,0:T(8,128)S(1)}, f32[4,256,128]{2,1,0:T(8,128)S(1)}, u32[]{:S(2)}, u32[]{:S(2)}) collective-permute-start(f32[4,256,128]{2,1,0:T(8,128)S(1)} %get-tuple-element.17), channel_id=1, source_target_pairs={{0,128},{1,129},{128,0},{129,1},{2,130},{3,131},{130,2},{131,3},{4... | collective-permute-start | bytes 1572872 | tf_op jit(solution)/shard_map/ppermute | solution.py:376
  91.8 0.6 collective-permute-start.13
  92.4 11.3 %collective-permute-done.11.refs_1_ = f32[4,256,128]{2,1,0:T(8,128)S(1)} collective-permute-done((f32[4,256,128]{2,1,0:T(8,128)S(1)}, f32[4,256,128]{2,1,0:T(8,128)S(1)}, u32[]{:S(2)}, u32[]{:S(2)}) %collective-permute-start.11) | collective-permute-done | bytes 524320 | tf_op jit(solution)/shard_map/ppermute | solution.py:376
  103.6 11.4 %collective-permute-done.12.refs_2_ = f32[4,256,128]{2,1,0:T(8,128)S(1)} collective-permute-done((f32[4,256,128]{2,1,0:T(8,128)S(1)}, f32[4,256,128]{2,1,0:T(8,128)S(1)}, u32[]{:S(2)}, u32[]{:S(2)}) %collective-permute-start.12) | collective-permute-done | bytes 524320 | tf_op jit(solution)/shard_map/ppermute | solution.py:376
  115.1 1.4 collective-permute-done.13.refs_3_
  116.4 4.9 %gram.1 = (f32[512,512]{1,0:T(8,128)}, f32[5,128,128]{2,1,0:T(8,128)S(1)}, f32[5,128,128]{2,1,0:T(8,128)S(1)}) custom-call(f32[4,256,128]{2,1,0:T(8,128)S(1)} %get-tuple-element.15.refs_0_, f32[4,256,128]{2,1,0:T(8,128)S(1)} %collective-permute-done.11.refs_1_, f32[4,256,128]{2,1,0:T(8,128)S(1)} %collective-permute-done.12.refs_2_, ...), custom_call_target="tpu_custom_call" | custom-call | tf_op jit(solution)/shard_map/gram/pallas_call | solution.py:191
  121.3 0.0 all-gather.3.cloned.1.call-update
  121.3 0.1 collective-permute-start.14
  121.4 1.6 collective-permute-done.14
  123.0 0.1 add.47
  123.1 16.2 %all_to_all.27 = f32[16,40,128]{2,1,0:T(8,128)S(1)} all-to-all(f32[16,40,128]{2,1,0:T(8,128)S(1)} %bitcast.41), channel_id=1, replica_groups=mesh['row'=2,'z'=8,'y'=4,'core'=2,'sk'=2] {'row','y','sk'}, dimensions={0} | all-to-all | bytes 655360 | tf_op jit(solution)/shard_map/all_to_all | solution.py:380
  139.3 11.8 %all_to_all.28 = f32[8,40,128]{2,1,0:T(8,128)S(1)} all-to-all(f32[8,40,128]{2,1,0:T(8,128)S(1)} %broadcast_in_dim.7), channel_id=1, replica_groups=mesh['row'=2,'z'=8,'y'=4,'core'=2,'sk'=2] {'z'}, dimensions={0} | all-to-all | bytes 327680 | tf_op jit(solution)/shard_map/all_to_all | solution.py:380
  151.2 16.1 %all_to_all.29 = f32[16,40,128]{2,1,0:T(8,128)S(1)} all-to-all(f32[16,40,128]{2,1,0:T(8,128)S(1)} %broadcast_in_dim.8), channel_id=1, replica_groups=mesh['row'=2,'z'=8,'y'=4,'core'=2,'sk'=2] {'row','y','sk'}, dimensions={0} | all-to-all | bytes 655360 | tf_op jit(solution)/shard_map/all_to_all | solution.py:380
  167.3 0.0 collective-permute-start.15
  167.3 1.6 collective-permute-done.15.other
  168.9 17.5 %cholesky.1 = (f32[512,512]{1,0:T(8,128)}, f32[512,512]{1,0:T(8,128)S(1)}) custom-call(f32[5,128,128]{2,1,0:T(8,128)S(1)} %bitcast.28, f32[5,128,128]{2,1,0:T(8,128)S(1)} %collective-permute-done.15.other), custom_call_target="tpu_custom_call" | custom-call | tf_op jit(solution)/shard_map/cholesky/pallas_call | solution.py:313
  186.4 0.0 all-gather.3.cloned.1.call-done
  186.4 0.0 copy-start
  186.4 2.2 %copy-done = f32[2048,512]{1,0:T(8,128)S(1)} copy-done((f32[2048,512]{1,0:T(8,128)S(1)}, f32[2048,512]{1,0:T(8,128)}, u32[]{:S(2)}) %copy-start) | copy-done | bytes 4194328
  188.6 4.1 %basis.1 = f32[2048,256]{1,0:T(8,128)} custom-call(f32[512,512]{1,0:T(8,128)S(1)} %get-tuple-element.21.inverse, f32[4,512,512]{2,1,0:T(8,128)S(1)} %bitcast.26), custom_call_target="tpu_custom_call" | custom-call | tf_op jit(solution)/shard_map/basis/pallas_call | solution.py:350
  (7 shorter events, 0.1 us)
Async XLA Ops:
  7.2 179.3 %all-gather.3.cloned.1.call-start = ((), (), s32[]{:S(2)}) async-start(), calls=%async_computation.5 | async-start | bytes 5242880 | tf_op jit(solution)/shard_map/all_gather | solution.py:413
  7.9 1.2 copy-start.1
  9.1 0.7 copy-start.2
  9.7 0.7 copy-start.4
  15.0 68.9 %copy-start.3 = (s32[1,1,4]{2,1,0:T(1,128)S(1)}, s32[1,1,4]{2,1,0:T(1,128)}, u32[]{:S(2)}) copy-start(s32[1,1,4]{2,1,0:T(1,128)} %param.6) | copy-start | bytes 52
  15.0 68.9 %copy-start.5 = (s32[1,1,4]{2,1,0:T(1,128)S(1)}, s32[1,1,4]{2,1,0:T(1,128)}, u32[]{:S(2)}) copy-start(s32[1,1,4]{2,1,0:T(1,128)} %param.7) | copy-start | bytes 52
  15.0 2.7 %collective-permute-start = (f32[4,2,256,128]{3,2,1,0:T(8,128)S(1)}, f32[4,2,256,128]{3,2,1,0:T(8,128)S(1)}, u32[]{:S(2)}, u32[]{:S(2)}) collective-permute-start(f32[4,2,256,128]{3,2,1,0:T(8,128)S(1)} %get-tuple-element.14), channel_id=1, source_target_pairs={{0,2},{2,0},{1,3},{3,1},{4,6},{6,4},{5,7},{7,5},{8,10},{10,8},{9,1... | collective-permute-start | bytes 3145736 | tf_op jit(solution)/shard_map/ppermute | solution.py:367
  17.9 10.1 %collective-permute-start.1 = (f32[2,256,128]{2,1,0:T(8,128)S(1)}, f32[2,256,128]{2,1,0:T(8,128)S(1)}, u32[]{:S(2)}, u32[]{:S(2)}) collective-permute-start(f32[2,256,128]{2,1,0:T(8,128)S(1)} %get-tuple-element.24), channel_id=1, source_target_pairs={{0,4},{4,8},{8,12},{12,0},{1,5},{5,9},{9,13},{13,1},{2,6},{6,10},{... | collective-permute-start | bytes 786440 | tf_op jit(solution)/shard_map/ppermute | solution.py:372
  19.7 15.1 %collective-permute-start.3 = (f32[2,256,128]{2,1,0:T(8,128)S(1)}, f32[2,256,128]{2,1,0:T(8,128)S(1)}, u32[]{:S(2)}, u32[]{:S(2)}) collective-permute-start(f32[2,256,128]{2,1,0:T(8,128)S(1)} %get-tuple-element.25), channel_id=1, source_target_pairs={{0,8},{4,12},{8,0},{12,4},{1,9},{5,13},{9,1},{13,5},{2,10},{6,14},... | collective-permute-start | bytes 786440 | tf_op jit(solution)/shard_map/ppermute | solution.py:372
  22.6 12.2 %collective-permute-start.2 = (f32[2,256,128]{2,1,0:T(8,128)S(1)}, f32[2,256,128]{2,1,0:T(8,128)S(1)}, u32[]{:S(2)}, u32[]{:S(2)}) collective-permute-start(f32[2,256,128]{2,1,0:T(8,128)S(1)} %get-tuple-element.26), channel_id=1, source_target_pairs={{0,12},{4,0},{8,4},{12,8},{1,13},{5,1},{9,5},{13,9},{2,14},{6,2},{... | collective-permute-start | bytes 786440 | tf_op jit(solution)/shard_map/ppermute | solution.py:372
  67.3 11.7 %collective-permute-start.6 = (f32[2,256,128]{2,1,0:T(8,128)S(1)}, f32[2,256,128]{2,1,0:T(8,128)S(1)}, u32[]{:S(2)}, u32[]{:S(2)}) collective-permute-start(f32[2,256,128]{2,1,0:T(8,128)S(1)} %bitcast.30), channel_id=1, source_target_pairs={{0,12},{4,0},{8,4},{12,8},{1,13},{5,1},{9,5},{13,9},{2,14},{6,2},{... | collective-permute-start | bytes 786440 | tf_op jit(solution)/shard_map/ppermute | solution.py:372
  70.7 9.4 %collective-permute-start.5 = (f32[2,256,128]{2,1,0:T(8,128)S(1)}, f32[2,256,128]{2,1,0:T(8,128)S(1)}, u32[]{:S(2)}, u32[]{:S(2)}) collective-permute-start(f32[2,256,128]{2,1,0:T(8,128)S(1)} %bitcast.31), channel_id=1, source_target_pairs={{0,8},{4,12},{8,0},{12,4},{1,9},{5,13},{9,1},{13,5},{2,10},{6,14},... | collective-permute-start | bytes 786440 | tf_op jit(solution)/shard_map/ppermute | solution.py:372
  71.0 11.4 %collective-permute-start.4 = (f32[2,256,128]{2,1,0:T(8,128)S(1)}, f32[2,256,128]{2,1,0:T(8,128)S(1)}, u32[]{:S(2)}, u32[]{:S(2)}) collective-permute-start(f32[2,256,128]{2,1,0:T(8,128)S(1)} %bitcast.32), channel_id=1, source_target_pairs={{0,4},{4,8},{8,12},{12,0},{1,5},{5,9},{9,13},{13,1},{2,6},{6,10},{... | collective-permute-start | bytes 786440 | tf_op jit(solution)/shard_map/ppermute | solution.py:372
  71.5 10.9 %collective-permute-start.7 = (f32[2,256,128]{2,1,0:T(8,128)S(1)}, f32[2,256,128]{2,1,0:T(8,128)S(1)}, u32[]{:S(2)}, u32[]{:S(2)}) collective-permute-start(f32[2,256,128]{2,1,0:T(8,128)S(1)} %bitcast.33), channel_id=1, source_target_pairs={{0,2},{2,0},{1,3},{3,1},{4,6},{6,4},{5,7},{7,5},{8,10},{10,8},{9,1... | collective-permute-start | bytes 786440 | tf_op jit(solution)/shard_map/ppermute | solution.py:367
  79.0 3.4 %collective-permute-start.10 = (f32[2,256,128]{2,1,0:T(8,128)S(1)}, f32[2,256,128]{2,1,0:T(8,128)S(1)}, u32[]{:S(2)}, u32[]{:S(2)}) collective-permute-start(f32[2,256,128]{2,1,0:T(8,128)S(1)} %collective-permute-done.6.rest_3_), channel_id=1, source_target_pairs={{0,2},{2,0},{1,3},{3,1},{4,6},{6,4},{5,7},{7,5},{8,10},{10,8},{9,1... | collective-permute-start | bytes 786440 | tf_op jit(solution)/shard_map/ppermute | solution.py:367
  80.0 2.4 %collective-permute-start.9 = (f32[2,256,128]{2,1,0:T(8,128)S(1)}, f32[2,256,128]{2,1,0:T(8,128)S(1)}, u32[]{:S(2)}, u32[]{:S(2)}) collective-permute-start(f32[2,256,128]{2,1,0:T(8,128)S(1)} %collective-permute-done.5.rest_2_), channel_id=1, source_target_pairs={{0,2},{2,0},{1,3},{3,1},{4,6},{6,4},{5,7},{7,5},{8,10},{10,8},{9,1... | collective-permute-start | bytes 786440 | tf_op jit(solution)/shard_map/ppermute | solution.py:367
  82.4 1.5 collective-permute-start.8
  88.8 14.9 %collective-permute-start.11 = (f32[4,256,128]{2,1,0:T(8,128)S(1)}, f32[4,256,128]{2,1,0:T(8,128)S(1)}, u32[]{:S(2)}, u32[]{:S(2)}) collective-permute-start(f32[4,256,128]{2,1,0:T(8,128)S(1)} %get-tuple-element.16), channel_id=1, source_target_pairs={{0,1},{1,0},{128,129},{129,128},{2,3},{3,2},{130,131},{131,130},{4... | collective-permute-start | bytes 1572872 | tf_op jit(solution)/shard_map/ppermute | solution.py:376
  89.4 25.7 %collective-permute-start.12 = (f32[4,256,128]{2,1,0:T(8,128)S(1)}, f32[4,256,128]{2,1,0:T(8,128)S(1)}, u32[]{:S(2)}, u32[]{:S(2)}) collective-permute-start(f32[4,256,128]{2,1,0:T(8,128)S(1)} %get-tuple-element.17), channel_id=1, source_target_pairs={{0,128},{1,129},{128,0},{129,1},{2,130},{3,131},{130,2},{131,3},{4... | collective-permute-start | bytes 1572872 | tf_op jit(solution)/shard_map/ppermute | solution.py:376
  91.8 24.6 %collective-permute-start.13 = (f32[4,256,128]{2,1,0:T(8,128)S(1)}, f32[4,256,128]{2,1,0:T(8,128)S(1)}, u32[]{:S(2)}, u32[]{:S(2)}) collective-permute-start(f32[4,256,128]{2,1,0:T(8,128)S(1)} %get-tuple-element.18), channel_id=1, source_target_pairs={{0,129},{1,128},{128,1},{129,0},{2,131},{3,130},{130,3},{131,2},{4... | collective-permute-start | bytes 1572872 | tf_op jit(solution)/shard_map/ppermute | solution.py:376
  121.3 1.7 collective-permute-start.14
  167.3 1.6 collective-permute-start.15
  186.4 2.2 %copy-start = (f32[2048,512]{1,0:T(8,128)S(1)}, f32[2048,512]{1,0:T(8,128)}, u32[]{:S(2)}) copy-start(f32[2048,512]{1,0:T(8,128)} %all-gather.3.cloned.1.call-done) | copy-start | bytes 12582916
Sparse Core Ops, SparseCore 0:
  121.4 50.7 all-gather.2

commit v3 on v2

--- a/solution.py
+++ b/solution.py
@@ -11,8 +11,9 @@
 F32 = jnp.float32
 BF16 = jnp.bfloat16
 RING = ("row", "sk")
+ODD = (1, 3)
 SHEET = ("row", "y", "sk")
-LIMIT = 48 * 1024 * 1024
+MIB = 1024 * 1024
 SIDE = 128
 GROUP = 8
 SUB = 32
@@ -37,17 +38,10 @@
         ]
         for s in range(slots)
     ]
-    for slot in copies[:2]:
+    for slot in copies:
         for copy in slot:
             copy.start()
     return copies
-
-
-def await_tile(copies, s):
-    for copy in copies[s]:
-        copy.wait()
-    for copy in copies[s + 2] if s + 2 < len(copies) else []:
-        copy.start()
 
 
 def forward_kernel(rows, cols, count, tiles, sketch, keep, send, held, sems):
@@ -59,7 +53,8 @@
     keep[...] = jnp.zeros_like(keep)
     send[...] = jnp.zeros_like(send)
     for s in range(slots):
-        await_tile(copies, s)
+        for copy in copies[s]:
+            copy.wait()
 
         def add(out):
             prod = dot(held[s], sketch[cols[s]], ((1,), (0,)))
@@ -92,7 +87,7 @@
         out_specs=[VMEM, VMEM],
         out_shape=[half, half],
         scratch_shapes=[pltpu.VMEM(tiles.shape, BF16), pltpu.SemaphoreType.DMA((slots, PARTS))],
-        compiler_params=pltpu.CompilerParams(vmem_limit_bytes=LIMIT),
+        compiler_params=pltpu.CompilerParams(vmem_limit_bytes=48 * MIB),
         name="forward",
     )(rows, cols, count, tiles, sketch)
 
@@ -115,7 +110,8 @@
             for h in range(piece.shape[0]):
                 flat[block, h * SIDE : (h + 1) * SIDE, here_part] = piece[h].astype(BF16).T
     for s in range(slots):
-        await_tile(copies, s)
+        for copy in copies[s]:
+            copy.wait()
 
         @pl.when(s < count[0])
         def _():
@@ -144,7 +140,7 @@
             pltpu.VMEM(tiles.shape, BF16),
             pltpu.SemaphoreType.DMA((slots, PARTS)),
         ],
-        compiler_params=pltpu.CompilerParams(vmem_limit_bytes=LIMIT),
+        compiler_params=pltpu.CompilerParams(vmem_limit_bytes=48 * MIB),
         name="backward",
     )(rows, cols, count, tiles, *own, *other)
 
@@ -154,7 +150,7 @@
 
 
 def gram_kernel(*refs):
-    zt, keep, send = refs[-3:]
+    low, high, keep, send, zt = refs[-5:]
     core = lax.axis_index("core")
     sk = lax.axis_index("sk")
     parts = refs[0:4]
@@ -163,6 +159,8 @@
         rows = pl.ds(pl.multiple_of((sk ^ far) * narrow, narrow), narrow)
         for n in range(chunks):
             zt[rows, n * SIDE : (n + 1) * SIDE] = parts[far][n] + parts[far + 2][n]
+    low[...] = zt[0:narrow, :]
+    high[...] = zt[narrow:, :]
     width = zt.shape[0]
     pairs = block_pairs(width // SIDE)
     half = len(pairs) // 2
@@ -191,9 +189,10 @@
     return pl.pallas_call(
         gram_kernel,
         in_specs=[VMEM] * len(parts),
-        out_specs=[VMEM] * 3,
-        out_shape=[jax.ShapeDtypeStruct((width, chunks * SIDE), F32), blocks, blocks],
-        compiler_params=pltpu.CompilerParams(vmem_limit_bytes=LIMIT),
+        out_specs=[VMEM] * 4,
+        out_shape=[jax.ShapeDtypeStruct((deep, chunks * SIDE), F32)] * 2 + [blocks, blocks],
+        scratch_shapes=[pltpu.VMEM((width, chunks * SIDE), F32)],
+        compiler_params=pltpu.CompilerParams(vmem_limit_bytes=32 * MIB),
         name="gram",
     )(*parts)
 
@@ -314,7 +313,8 @@
         functools.partial(cholesky_kernel, 1.0 / total_rows),
         out_shape=[square, square],
         scratch_shapes=[pltpu.VMEM((SIDE, 2 * SIDE), F32)],
-        compiler_params=pltpu.CompilerParams(vmem_limit_bytes=LIMIT),
+        compiler_params=pltpu.CompilerParams(vmem_limit_bytes=24 * MIB),
+        cost_estimate=pl.CostEstimate(flops=2**34, bytes_accessed=2**22, transcendentals=0),
         name="cholesky",
     )(own, other)
 
@@ -324,43 +324,39 @@
     return high, (x - high.astype(F32)).astype(BF16)
 
 
-def basis_kernel(inverse, quarters, out, held, done, load, store):
+def basis_kernel(inverse, *refs):
+    lows, highs = refs[0:4], refs[4:8]
+    out, done, store = refs[8:]
+    here = 2 * lax.axis_index("row") + lax.axis_index("sk")
     chunk, narrow = done.shape[1:]
-    loads = [pltpu.make_async_copy(quarters.at[n], held.at[n], load.at[n]) for n in range(4)]
-    for copy in loads:
-        copy.start()
-    w = inverse[pl.ds(pl.multiple_of(lax.axis_index("sk") * narrow, narrow), narrow), :]
-    w_high, w_low = split(w)
+    form = ((1,), (0,))
+    rows = pl.ds(pl.multiple_of(lax.axis_index("sk") * narrow, narrow), narrow)
+    weights = [split(inverse[rows, k * narrow : (k + 1) * narrow]) for k in range(2)]
     stores = []
     for n in range(4):
-        loads[n].wait()
-        high, low = split(held[n])
-        form = ((1,), (0,))
-        done[n] = (dot(w_high, high, form) + (dot(w_high, low, form) + dot(w_low, high, form))).T
-        stores.append(pltpu.make_async_copy(done.at[n], out.at[pl.ds(n * chunk, chunk), :], store.at[n]))
+        total = 0.0
+        for (w_high, w_low), part in zip(weights, (lows[n], highs[n])):
+            high, low = split(part[...])
+            total += dot(w_high, high, form) + (dot(w_high, low, form) + dot(w_low, high, form))
+        done[n] = total.T
+        place = pl.ds(pl.multiple_of((here ^ n) * chunk, chunk), chunk)
+        stores.append(pltpu.make_async_copy(done.at[n], out.at[place, :], store.at[n]))
         stores[n].start()
     for copy in stores:
         copy.wait()
 
 
-def basis_of(inverse, quarters):
-    width = inverse.shape[0]
-    narrow = width // 2
-    chunk = quarters.shape[2]
+def basis_of(inverse, lows, highs):
+    narrow, chunk = lows[0].shape
     return pl.pallas_call(
         basis_kernel,
-        in_specs=[VMEM, ANY],
+        in_specs=[VMEM] * 9,
         out_specs=ANY,
         out_shape=jax.ShapeDtypeStruct((4 * chunk, narrow), F32),
-        scratch_shapes=[
-            pltpu.VMEM((4, width, chunk), F32),
-            pltpu.VMEM((4, chunk, narrow), F32),
-            pltpu.SemaphoreType.DMA((4,)),
-            pltpu.SemaphoreType.DMA((4,)),
-        ],
-        compiler_params=pltpu.CompilerParams(vmem_limit_bytes=LIMIT),
+        scratch_shapes=[pltpu.VMEM((4, chunk, narrow), F32), pltpu.SemaphoreType.DMA((4,))],
+        compiler_params=pltpu.CompilerParams(vmem_limit_bytes=32 * MIB),
         name="basis",
-    )(inverse, quarters)
+    )(inverse, *lows, *highs)
 
 
 def swap(x):
@@ -372,8 +368,8 @@
     return lax.ppermute(x, axes, [(i, (i + n) % size) for i in range(size)])
 
 
-def across(x, n):
-    return lax.ppermute(x, RING, [(i, i ^ n) for i in range(4)])
+def across(x, n, to=range(4)):
+    return lax.ppermute(x, RING, [(i ^ n, i) for i in to])
 
 
 def exchange(x, axes):
@@ -409,19 +405,25 @@
     other = [swap(p) for p in own]
     pieces = backward(rows, cols, count, blocks, own, other)
     moved = [pieces[0]] + [across(pieces[n], n) for n in range(1, 4)]
-    zt, keep, send = gram_of(moved)
-    quarters = lax.all_gather(zt, RING, axis=0)
-
+    low, high, keep, send = gram_of(moved)
+
+    lows = [low, across(low, 1), None, across(low, 3)]
     half = keep + swap(send)
     sheet = lax.axis_size(SHEET)
     pieces = exchange(half.reshape(sheet, -1, SIDE), SHEET)
-    piece = jnp.sum(pieces, axis=0)
+    piece, lows[1], lows[3] = lax.optimization_barrier((jnp.sum(pieces, axis=0), lows[1], lows[3]))
+    late, _ = lax.optimization_barrier((high, piece))
+    highs = [high, across(late, 1, ODD), None, across(late, 3, ODD)]
     piece = jnp.sum(spread(piece, "z"), axis=0)
+    piece, highs[1], highs[3] = lax.optimization_barrier((piece, highs[1], highs[3]))
     own_g = spread(piece, SHEET).reshape(keep.shape)
+    late, latest, _ = lax.optimization_barrier((low, high, own_g))
+    lows[2] = across(late, 2)
+    highs[2] = across(latest, 2, ODD)
     other_g = swap(own_g)
 
     upper, inverse = cholesky(own_g, other_g, total_rows, width)
-    return basis_of(inverse, quarters), upper
+    return basis_of(inverse, lows, highs), upper
 
 
 def solution(mesh):

time: 203 us -> 196 us (0.966); the launches traced: 200 us -> 196 us
  between operations: 14.8 us -> 1.67 us
  starting transfers between devices: 14 us -> 25.7 us
  waiting for transfers between devices: 53.4 us -> 56.3 us
  local copies, waits for them, and re-layouts: 4.78 us -> 2.59 us
    ppermute x3 -> x9, starting transfers between devices: 3.58 us -> 15 us  [across(): return lax.ppermute(x, RING, [(i ^ n, i) for i in to])]
    ppermute x3 -> x9, waiting for transfers between devices: 24.1 us -> 31.6 us  [across(): return lax.ppermute(x, RING, [(i ^ n, i) for i in to])]
    ppermute x7, waiting for transfers between devices: 7.41 us -> 4.17 us  [swap(): return lax.ppermute(x, 'core', [(0, 1), (1, 0)])]
    unnamed x12 -> x10, local copies, waits for them, and re-layouts: 4.73 us -> 2.54 us
  transfers between devices with their start and end apart: 17 -> 22, of which waited for: 12 -> 13; matrix products, arithmetic and copies ran while one was open for 0% -> 0% of each run, Pallas kernels for 9% -> 9%
where the time goes in v3:
time: 196 us
  blocking collectives  74.5 us (38%)
  waiting for transfers between devices  56.3 us (29%)
  Pallas kernels  34.6 us (18%)
  starting transfers between devices  25.7 us (13%)
  local copies, waits for them, and re-layouts  2.59 us (1%)
    all_to_all x5, blocking collectives, exchange(): return lax.all_to_all(x, axes, 0, 0, tiled=True)  74.5 us
    ppermute x9, waiting for transfers between devices, across(): return lax.ppermute(x, RING, [(i ^ n, i) for i in to])  31.6 us
    ppermute x6, waiting for transfers between devices, shift(): return lax.ppermute(x, axes, [(i, (i + n) % size) for i in range(size)])  20.6 us
    pallas_call x1, Pallas kernels, cholesky(): pl.pallas_call(functools.partial(cholesky_kernel, 1.0 / total_rows), out_...  17.5 us
    ppermute x9, starting transfers between devices, across(): return lax.ppermute(x, RING, [(i ^ n, i) for i in to])  15 us
    ppermute x6, starting transfers between devices, shift(): return lax.ppermute(x, axes, [(i, (i + n) % size) for i in range(size)])  10.5 us
    pallas_call x1, Pallas kernels, backward(): pl.pallas_call(backward_kernel, in_specs=[SMEM, SMEM, SMEM, ANY] + [VMEM]...  5.43 us
    pallas_call x1, Pallas kernels, forward(): pl.pallas_call(forward_kernel, in_specs=[SMEM, SMEM, SMEM, ANY, VMEM], ou...  5.16 us
  transfers between devices with their start and end apart: 22, of which 13 were waited for; matrix products, arithmetic and copies ran while one was open for 0% of the time, Pallas kernels for 9%

profile of v3, /device:TPU:2, one launch (start us, length us, event | category | flops | bytes accessed | tf_op | source)
XLA Modules:
  0.0 195.7 jit_solution(7287829051166655252)
XLA Ops:
  0.6 0.0 copy-start.4
  0.6 0.0 copy-start.2
  1.3 0.0 copy-start
  1.3 1.2 copy-done
  2.5 0.7 copy-done.1
  3.2 0.7 copy-done.3
  3.9 5.2 %forward.1 = (f32[4,2,256,128]{3,2,1,0:T(8,128)S(1)}, f32[4,2,256,128]{3,2,1,0:T(8,128)S(1)}) custom-call(s32[4]{0:T(128)S(1)} %bitcast.33, s32[4]{0:T(128)S(1)} %bitcast.35, s32[1]{0:T(128)} %bitcast.23.count, bf16[4,1024,1024]{2,1,0:T(8,128)(2,1)} %bitcast.37, bf16[2,1024,256]{2,1,0:T(8,128)(2,1)S(1)} %bitcast.25), custom_call_target="tpu_custom_call" | custom-call | tf_op jit(solution)/shard_map/forward/pallas_call | solution.py:84
  9.0 0.1 collective-permute-start
  9.1 2.6 %collective-permute-done = f32[4,2,256,128]{3,2,1,0:T(8,128)S(1)} collective-permute-done((f32[4,2,256,128]{3,2,1,0:T(8,128)S(1)}, f32[4,2,256,128]{3,2,1,0:T(8,128)S(1)}, u32[]{:S(2)}, u32[]{:S(2)}) %collective-permute-start) | collective-permute-done | bytes 1048608 | tf_op jit(solution)/shard_map/ppermute | solution.py:363
  11.8 0.1 fusion.2
  11.9 1.1 collective-permute-start.1
  13.0 2.9 %collective-permute-start.3 = (f32[2,256,128]{2,1,0:T(8,128)S(1)}, f32[2,256,128]{2,1,0:T(8,128)S(1)}, u32[]{:S(2)}, u32[]{:S(2)}) collective-permute-start(f32[2,256,128]{2,1,0:T(8,128)S(1)} %get-tuple-element.45), channel_id=1, source_target_pairs={{0,8},{4,12},{8,0},{12,4},{1,9},{5,13},{9,1},{13,5},{2,10},{6,14},... | collective-permute-start | bytes 786440 | tf_op jit(solution)/shard_map/ppermute | solution.py:368
  15.9 1.9 collective-permute-start.2
  17.8 3.7 %collective-permute-done.1 = f32[2,256,128]{2,1,0:T(8,128)S(1)} collective-permute-done((f32[2,256,128]{2,1,0:T(8,128)S(1)}, f32[2,256,128]{2,1,0:T(8,128)S(1)}, u32[]{:S(2)}, u32[]{:S(2)}) %collective-permute-start.1) | collective-permute-done | bytes 262176 | tf_op jit(solution)/shard_map/ppermute | solution.py:368
  21.5 6.6 %collective-permute-done.3 = f32[2,256,128]{2,1,0:T(8,128)S(1)} collective-permute-done((f32[2,256,128]{2,1,0:T(8,128)S(1)}, f32[2,256,128]{2,1,0:T(8,128)S(1)}, u32[]{:S(2)}, u32[]{:S(2)}) %collective-permute-start.3) | collective-permute-done | bytes 262176 | tf_op jit(solution)/shard_map/ppermute | solution.py:368
  28.1 0.0 collective-permute-done.2
  28.1 0.1 fusion.6
  28.1 19.0 %all_to_all.25 = f32[8,64,128]{2,1,0:T(8,128)S(1)} all-to-all(f32[8,64,128]{2,1,0:T(8,128)S(1)} %bitcast.40), channel_id=1, replica_groups=mesh['row'=2,'z'=8,'y'=4,'core'=2,'sk'=2] {'z'}, dimensions={0} | all-to-all | bytes 524288 | tf_op jit(solution)/shard_map/all_to_all | solution.py:376
  47.2 12.9 %all_to_all.26 = f32[8,64,128]{2,1,0:T(8,128)S(1)} all-to-all(f32[8,64,128]{2,1,0:T(8,128)S(1)} %broadcast_in_dim.6), channel_id=1, replica_groups=mesh['row'=2,'z'=8,'y'=4,'core'=2,'sk'=2] {'z'}, dimensions={0} | all-to-all | bytes 524288 | tf_op jit(solution)/shard_map/all_to_all | solution.py:376
  60.1 3.2 %collective-permute-start.6 = (f32[2,256,128]{2,1,0:T(8,128)S(1)}, f32[2,256,128]{2,1,0:T(8,128)S(1)}, u32[]{:S(2)}, u32[]{:S(2)}) collective-permute-start(f32[2,256,128]{2,1,0:T(8,128)S(1)} %bitcast.26), channel_id=1, source_target_pairs={{0,12},{4,0},{8,4},{12,8},{1,13},{5,1},{9,5},{13,9},{2,14},{6,2},{... | collective-permute-start | bytes 786440 | tf_op jit(solution)/shard_map/ppermute | solution.py:368
  63.2 0.0 collective-permute-start.5
  63.3 1.4 collective-permute-start.4
  64.7 0.0 collective-permute-start.7
  64.7 6.9 %collective-permute-done.6.rest_3_ = f32[2,256,128]{2,1,0:T(8,128)S(1)} collective-permute-done((f32[2,256,128]{2,1,0:T(8,128)S(1)}, f32[2,256,128]{2,1,0:T(8,128)S(1)}, u32[]{:S(2)}, u32[]{:S(2)}) %collective-permute-start.6) | collective-permute-done | bytes 262176 | tf_op jit(solution)/shard_map/ppermute | solution.py:368
  71.6 0.0 collective-permute-start.10
  71.6 1.0 collective-permute-done.5.rest_2_
  72.6 0.0 collective-permute-start.9
  72.6 2.4 %collective-permute-done.4.rest_1_ = f32[2,256,128]{2,1,0:T(8,128)S(1)} collective-permute-done((f32[2,256,128]{2,1,0:T(8,128)S(1)}, f32[2,256,128]{2,1,0:T(8,128)S(1)}, u32[]{:S(2)}, u32[]{:S(2)}) %collective-permute-start.4) | collective-permute-done | bytes 262176 | tf_op jit(solution)/shard_map/ppermute | solution.py:368
  75.0 0.0 collective-permute-start.8
  75.0 0.0 collective-permute-done.7.rest_4_
  75.0 0.0 collective-permute-done.10.rest_7_
  75.0 0.0 collective-permute-done.9.rest_6_
  75.0 1.5 collective-permute-done.8.rest_5_
  76.5 0.0 copy-done.4
  76.5 0.0 copy-done.2
  76.5 5.4 %backward.1 = (f32[4,256,128]{2,1,0:T(8,128)S(1)}, f32[4,256,128]{2,1,0:T(8,128)S(1)}, f32[4,256,128]{2,1,0:T(8,128)S(1)}, f32[4,256,128]{2,1,0:T(8,128)S(1)}) custom-call(s32[4]{0:T(128)S(1)} %bitcast.34, s32[4]{0:T(128)S(1)} %bitcast.36, s32[1]{0:T(128)} %bitcast.24.count, bf16[4,1024,1024]{2,1,0:T(8,128)(2,1)} %bitcast.38, f32[2,256,128]{2,1,0:T(8,128)S(1)} %bitcast.30, ...), custom_call_target="tpu_custom_call" | custom-call | tf_op jit(solution)/shard_map/backward/pallas_call | solution.py:132
  82.0 0.6 collective-permute-start.11
  82.6 2.3 %collective-permute-start.12 = (f32[4,256,128]{2,1,0:T(8,128)S(1)}, f32[4,256,128]{2,1,0:T(8,128)S(1)}, u32[]{:S(2)}, u32[]{:S(2)}) collective-permute-start(f32[4,256,128]{2,1,0:T(8,128)S(1)} %get-tuple-element.27), channel_id=1, source_target_pairs={{128,0},{129,1},{0,128},{1,129},{130,2},{131,3},{2,130},{3,131},{1... | collective-permute-start | bytes 1572872 | tf_op jit(solution)/shard_map/ppermute | solution.py:372
  84.9 0.6 collective-permute-start.13
  85.5 11.4 %collective-permute-done.11.refs_1_ = f32[4,256,128]{2,1,0:T(8,128)S(1)} collective-permute-done((f32[4,256,128]{2,1,0:T(8,128)S(1)}, f32[4,256,128]{2,1,0:T(8,128)S(1)}, u32[]{:S(2)}, u32[]{:S(2)}) %collective-permute-start.11) | collective-permute-done | bytes 524320 | tf_op jit(solution)/shard_map/ppermute | solution.py:372
  96.9 12.0 %collective-permute-done.12.refs_2_ = f32[4,256,128]{2,1,0:T(8,128)S(1)} collective-permute-done((f32[4,256,128]{2,1,0:T(8,128)S(1)}, f32[4,256,128]{2,1,0:T(8,128)S(1)}, u32[]{:S(2)}, u32[]{:S(2)}) %collective-permute-start.12) | collective-permute-done | bytes 524320 | tf_op jit(solution)/shard_map/ppermute | solution.py:372
  108.9 1.4 collective-permute-done.13.refs_3_
  110.3 3.8 %gram.1 = (f32[256,512]{1,0:T(8,128)S(1)}, f32[256,512]{1,0:T(8,128)S(1)}, f32[5,128,128]{2,1,0:T(8,128)S(1)}, f32[5,128,128]{2,1,0:T(8,128)S(1)}) custom-call(f32[4,256,128]{2,1,0:T(8,128)S(1)} %get-tuple-element.25.refs_0_, f32[4,256,128]{2,1,0:T(8,128)S(1)} %collective-permute-done.11.refs_1_, f32[4,256,128]{2,1,0:T(8,128)S(1)} %collective-permute-done.12.refs_2_, ...), custom_call_target="tpu_custom_call" | custom-call | tf_op jit(solution)/shard_map/gram/pallas_call | solution.py:189
  114.1 0.1 collective-permute-start.14
  114.2 0.4 collective-permute-start.16
  114.5 3.0 %collective-permute-start.15 = (f32[256,512]{1,0:T(8,128)S(1)}, f32[256,512]{1,0:T(8,128)S(1)}, u32[]{:S(2)}, u32[]{:S(2)}) collective-permute-start(f32[256,512]{1,0:T(8,128)S(1)} %get-tuple-element.38.refs_0_), channel_id=1, source_target_pairs={{1,0},{0,1},{129,128},{128,129},{3,2},{2,3},{131,130},{130,131},{5... | collective-permute-start | bytes 1572872 | tf_op jit(solution)/shard_map/ppermute | solution.py:372
  117.5 0.0 collective-permute-done.14
  117.6 16.9 %all_to_all.27 = f32[16,40,128]{2,1,0:T(8,128)S(1)} all-to-all(f32[16,40,128]{2,1,0:T(8,128)S(1)} %bitcast.39), channel_id=1, replica_groups=mesh['row'=2,'z'=8,'y'=4,'core'=2,'sk'=2] {'row','y','sk'}, dimensions={0} | all-to-all | bytes 655360 | tf_op jit(solution)/shard_map/all_to_all | solution.py:376
  134.5 0.0 collective-permute-done.16.refs_3_
  134.5 0.0 collective-permute-done.15.refs_1_
  134.6 1.3 collective-permute-start.18
  135.9 1.3 collective-permute-start.17
  137.2 11.9 %all_to_all.28 = f32[8,40,128]{2,1,0:T(8,128)S(1)} all-to-all(f32[8,40,128]{2,1,0:T(8,128)S(1)} %broadcast_in_dim.7), channel_id=1, replica_groups=mesh['row'=2,'z'=8,'y'=4,'core'=2,'sk'=2] {'z'}, dimensions={0} | all-to-all | bytes 327680 | tf_op jit(solution)/shard_map/all_to_all | solution.py:376
  149.1 0.5 collective-permute-done.18.refs_7_
  149.6 2.2 %collective-permute-done.17.refs_5_ = f32[256,512]{1,0:T(8,128)S(1)} collective-permute-done((f32[256,512]{1,0:T(8,128)S(1)}, f32[256,512]{1,0:T(8,128)S(1)}, u32[]{:S(2)}, u32[]{:S(2)}) %collective-permute-start.17) | collective-permute-done | bytes 524320 | tf_op jit(solution)/shard_map/ppermute | solution.py:372
  151.8 13.8 %all_to_all.29 = f32[16,40,128]{2,1,0:T(8,128)S(1)} all-to-all(f32[16,40,128]{2,1,0:T(8,128)S(1)} %broadcast_in_dim.8), channel_id=1, replica_groups=mesh['row'=2,'z'=8,'y'=4,'core'=2,'sk'=2] {'row','y','sk'}, dimensions={0} | all-to-all | bytes 655360 | tf_op jit(solution)/shard_map/all_to_all | solution.py:376
  165.6 0.0 collective-permute-start.19
  165.6 1.5 collective-permute-start.20
  167.1 4.0 %collective-permute-start.21 = (f32[256,512]{1,0:T(8,128)S(1)}, f32[256,512]{1,0:T(8,128)S(1)}, u32[]{:S(2)}, u32[]{:S(2)}) collective-permute-start(f32[256,512]{1,0:T(8,128)S(1)} %get-tuple-element.41.refs_4_), channel_id=1, source_target_pairs={{129,1},{1,129},{131,3},{3,131},{133,5},{5,133},{135,7},{7,135},{1... | collective-permute-start | bytes 1572872 | tf_op jit(solution)/shard_map/ppermute | solution.py:372
  171.0 0.0 collective-permute-done.19.other
  171.0 17.5 %cholesky.1 = (f32[512,512]{1,0:T(8,128)}, f32[512,512]{1,0:T(8,128)S(1)}) custom-call(f32[5,128,128]{2,1,0:T(8,128)S(1)} %bitcast.32, f32[5,128,128]{2,1,0:T(8,128)S(1)} %collective-permute-done.19.other), custom_call_target="tpu_custom_call" | custom-call | flops 17179869184 | bytes 4194304 | tf_op jit(solution)/shard_map/cholesky/pallas_call | solution.py:312
  188.5 0.0 collective-permute-done.20.refs_2_
  188.5 4.1 %collective-permute-done.21.refs_6_ = f32[256,512]{1,0:T(8,128)S(1)} collective-permute-done((f32[256,512]{1,0:T(8,128)S(1)}, f32[256,512]{1,0:T(8,128)S(1)}, u32[]{:S(2)}, u32[]{:S(2)}) %collective-permute-start.21) | collective-permute-done | bytes 524320 | tf_op jit(solution)/shard_map/ppermute | solution.py:372
  192.7 2.8 %basis.1 = f32[2048,256]{1,0:T(8,128)} custom-call(f32[512,512]{1,0:T(8,128)S(1)} %get-tuple-element.36.inverse, f32[256,512]{1,0:T(8,128)S(1)} %get-tuple-element.38.refs_0_, f32[256,512]{1,0:T(8,128)S(1)} %collective-permute-done.15.refs_1_, f32[256,512]{1,0:T(8,128)S(1)} %collective-permute-done.20.refs_2_, ...), custom_call_target="tpu_custom_call" | custom-call | tf_op jit(solution)/shard_map/basis/pallas_call | solution.py:351
  (10 shorter events, 0.2 us)
Async XLA Ops:
  0.6 75.9 %copy-start.4 = (s32[1,1,4]{2,1,0:T(1,128)S(1)}, s32[1,1,4]{2,1,0:T(1,128)}, u32[]{:S(2)}) copy-start(s32[1,1,4]{2,1,0:T(1,128)} %param.7) | copy-start | bytes 52
  0.6 75.9 %copy-start.2 = (s32[1,1,4]{2,1,0:T(1,128)S(1)}, s32[1,1,4]{2,1,0:T(1,128)}, u32[]{:S(2)}) copy-start(s32[1,1,4]{2,1,0:T(1,128)} %param.6) | copy-start | bytes 52
  1.3 1.2 copy-start
  2.5 0.7 copy-start.1
  3.2 0.7 copy-start.3
  9.0 2.7 %collective-permute-start = (f32[4,2,256,128]{3,2,1,0:T(8,128)S(1)}, f32[4,2,256,128]{3,2,1,0:T(8,128)S(1)}, u32[]{:S(2)}, u32[]{:S(2)}) collective-permute-start(f32[4,2,256,128]{3,2,1,0:T(8,128)S(1)} %get-tuple-element.24), channel_id=1, source_target_pairs={{0,2},{2,0},{1,3},{3,1},{4,6},{6,4},{5,7},{7,5},{8,10},{10,8},{9,1... | collective-permute-start | bytes 3145736 | tf_op jit(solution)/shard_map/ppermute | solution.py:363
  11.9 9.6 %collective-permute-start.1 = (f32[2,256,128]{2,1,0:T(8,128)S(1)}, f32[2,256,128]{2,1,0:T(8,128)S(1)}, u32[]{:S(2)}, u32[]{:S(2)}) collective-permute-start(f32[2,256,128]{2,1,0:T(8,128)S(1)} %get-tuple-element.44), channel_id=1, source_target_pairs={{0,4},{4,8},{8,12},{12,0},{1,5},{5,9},{9,13},{13,1},{2,6},{6,10},{... | collective-permute-start | bytes 786440 | tf_op jit(solution)/shard_map/ppermute | solution.py:368
  13.0 15.1 %collective-permute-start.3 = (f32[2,256,128]{2,1,0:T(8,128)S(1)}, f32[2,256,128]{2,1,0:T(8,128)S(1)}, u32[]{:S(2)}, u32[]{:S(2)}) collective-permute-start(f32[2,256,128]{2,1,0:T(8,128)S(1)} %get-tuple-element.45), channel_id=1, source_target_pairs={{0,8},{4,12},{8,0},{12,4},{1,9},{5,13},{9,1},{13,5},{2,10},{6,14},... | collective-permute-start | bytes 786440 | tf_op jit(solution)/shard_map/ppermute | solution.py:368
  15.9 12.2 %collective-permute-start.2 = (f32[2,256,128]{2,1,0:T(8,128)S(1)}, f32[2,256,128]{2,1,0:T(8,128)S(1)}, u32[]{:S(2)}, u32[]{:S(2)}) collective-permute-start(f32[2,256,128]{2,1,0:T(8,128)S(1)} %get-tuple-element.46), channel_id=1, source_target_pairs={{0,12},{4,0},{8,4},{12,8},{1,13},{5,1},{9,5},{13,9},{2,14},{6,2},{... | collective-permute-start | bytes 786440 | tf_op jit(solution)/shard_map/ppermute | solution.py:368
  60.1 11.5 %collective-permute-start.6 = (f32[2,256,128]{2,1,0:T(8,128)S(1)}, f32[2,256,128]{2,1,0:T(8,128)S(1)}, u32[]{:S(2)}, u32[]{:S(2)}) collective-permute-start(f32[2,256,128]{2,1,0:T(8,128)S(1)} %bitcast.26), channel_id=1, source_target_pairs={{0,12},{4,0},{8,4},{12,8},{1,13},{5,1},{9,5},{13,9},{2,14},{6,2},{... | collective-permute-start | bytes 786440 | tf_op jit(solution)/shard_map/ppermute | solution.py:368
  63.2 9.4 %collective-permute-start.5 = (f32[2,256,128]{2,1,0:T(8,128)S(1)}, f32[2,256,128]{2,1,0:T(8,128)S(1)}, u32[]{:S(2)}, u32[]{:S(2)}) collective-permute-start(f32[2,256,128]{2,1,0:T(8,128)S(1)} %bitcast.27), channel_id=1, source_target_pairs={{0,8},{4,12},{8,0},{12,4},{1,9},{5,13},{9,1},{13,5},{2,10},{6,14},... | collective-permute-start | bytes 786440 | tf_op jit(solution)/shard_map/ppermute | solution.py:368
  63.3 11.7 %collective-permute-start.4 = (f32[2,256,128]{2,1,0:T(8,128)S(1)}, f32[2,256,128]{2,1,0:T(8,128)S(1)}, u32[]{:S(2)}, u32[]{:S(2)}) collective-permute-start(f32[2,256,128]{2,1,0:T(8,128)S(1)} %bitcast.28), channel_id=1, source_target_pairs={{0,4},{4,8},{8,12},{12,0},{1,5},{5,9},{9,13},{13,1},{2,6},{6,10},{... | collective-permute-start | bytes 786440 | tf_op jit(solution)/shard_map/ppermute | solution.py:368
  64.7 10.3 %collective-permute-start.7 = (f32[2,256,128]{2,1,0:T(8,128)S(1)}, f32[2,256,128]{2,1,0:T(8,128)S(1)}, u32[]{:S(2)}, u32[]{:S(2)}) collective-permute-start(f32[2,256,128]{2,1,0:T(8,128)S(1)} %bitcast.29), channel_id=1, source_target_pairs={{0,2},{2,0},{1,3},{3,1},{4,6},{6,4},{5,7},{7,5},{8,10},{10,8},{9,1... | collective-permute-start | bytes 786440 | tf_op jit(solution)/shard_map/ppermute | solution.py:363
  71.6 3.4 %collective-permute-start.10 = (f32[2,256,128]{2,1,0:T(8,128)S(1)}, f32[2,256,128]{2,1,0:T(8,128)S(1)}, u32[]{:S(2)}, u32[]{:S(2)}) collective-permute-start(f32[2,256,128]{2,1,0:T(8,128)S(1)} %collective-permute-done.6.rest_3_), channel_id=1, source_target_pairs={{0,2},{2,0},{1,3},{3,1},{4,6},{6,4},{5,7},{7,5},{8,10},{10,8},{9,1... | collective-permute-start | bytes 786440 | tf_op jit(solution)/shard_map/ppermute | solution.py:363
  72.6 2.4 %collective-permute-start.9 = (f32[2,256,128]{2,1,0:T(8,128)S(1)}, f32[2,256,128]{2,1,0:T(8,128)S(1)}, u32[]{:S(2)}, u32[]{:S(2)}) collective-permute-start(f32[2,256,128]{2,1,0:T(8,128)S(1)} %collective-permute-done.5.rest_2_), channel_id=1, source_target_pairs={{0,2},{2,0},{1,3},{3,1},{4,6},{6,4},{5,7},{7,5},{8,10},{10,8},{9,1... | collective-permute-start | bytes 786440 | tf_op jit(solution)/shard_map/ppermute | solution.py:363
  75.0 1.5 collective-permute-start.8
  82.0 15.0 %collective-permute-start.11 = (f32[4,256,128]{2,1,0:T(8,128)S(1)}, f32[4,256,128]{2,1,0:T(8,128)S(1)}, u32[]{:S(2)}, u32[]{:S(2)}) collective-permute-start(f32[4,256,128]{2,1,0:T(8,128)S(1)} %get-tuple-element.26), channel_id=1, source_target_pairs={{1,0},{0,1},{129,128},{128,129},{3,2},{2,3},{131,130},{130,131},{5... | collective-permute-start | bytes 1572872 | tf_op jit(solution)/shard_map/ppermute | solution.py:372
  82.6 26.3 %collective-permute-start.12 = (f32[4,256,128]{2,1,0:T(8,128)S(1)}, f32[4,256,128]{2,1,0:T(8,128)S(1)}, u32[]{:S(2)}, u32[]{:S(2)}) collective-permute-start(f32[4,256,128]{2,1,0:T(8,128)S(1)} %get-tuple-element.27), channel_id=1, source_target_pairs={{128,0},{129,1},{0,128},{1,129},{130,2},{131,3},{2,130},{3,131},{1... | collective-permute-start | bytes 1572872 | tf_op jit(solution)/shard_map/ppermute | solution.py:372
  84.9 25.4 %collective-permute-start.13 = (f32[4,256,128]{2,1,0:T(8,128)S(1)}, f32[4,256,128]{2,1,0:T(8,128)S(1)}, u32[]{:S(2)}, u32[]{:S(2)}) collective-permute-start(f32[4,256,128]{2,1,0:T(8,128)S(1)} %get-tuple-element.28), channel_id=1, source_target_pairs={{129,0},{128,1},{1,128},{0,129},{131,2},{130,3},{3,130},{2,131},{1... | collective-permute-start | bytes 1572872 | tf_op jit(solution)/shard_map/ppermute | solution.py:372
  114.1 3.5 %collective-permute-start.14 = (f32[5,128,128]{2,1,0:T(8,128)S(1)}, f32[5,128,128]{2,1,0:T(8,128)S(1)}, u32[]{:S(2)}, u32[]{:S(2)}) collective-permute-start(f32[5,128,128]{2,1,0:T(8,128)S(1)} %get-tuple-element.30), channel_id=1, source_target_pairs={{0,2},{2,0},{1,3},{3,1},{4,6},{6,4},{5,7},{7,5},{8,10},{10,8},{9,1... | collective-permute-start | bytes 983048 | tf_op jit(solution)/shard_map/ppermute | solution.py:363
  114.2 20.4 %collective-permute-start.16 = (f32[256,512]{1,0:T(8,128)S(1)}, f32[256,512]{1,0:T(8,128)S(1)}, u32[]{:S(2)}, u32[]{:S(2)}) collective-permute-start(f32[256,512]{1,0:T(8,128)S(1)} %get-tuple-element.38.refs_0_), channel_id=1, source_target_pairs={{129,0},{128,1},{1,128},{0,129},{131,2},{130,3},{3,130},{2,131},{1... | collective-permute-start | bytes 1572872 | tf_op jit(solution)/shard_map/ppermute | solution.py:372
  114.5 20.0 %collective-permute-start.15 = (f32[256,512]{1,0:T(8,128)S(1)}, f32[256,512]{1,0:T(8,128)S(1)}, u32[]{:S(2)}, u32[]{:S(2)}) collective-permute-start(f32[256,512]{1,0:T(8,128)S(1)} %get-tuple-element.38.refs_0_), channel_id=1, source_target_pairs={{1,0},{0,1},{129,128},{128,129},{3,2},{2,3},{131,130},{130,131},{5... | collective-permute-start | bytes 1572872 | tf_op jit(solution)/shard_map/ppermute | solution.py:372
  134.6 15.1 %collective-permute-start.18 = (f32[256,512]{1,0:T(8,128)S(1)}, f32[256,512]{1,0:T(8,128)S(1)}, u32[]{:S(2)}, u32[]{:S(2)}) collective-permute-start(f32[256,512]{1,0:T(8,128)S(1)} %get-tuple-element.41.refs_4_), channel_id=1, source_target_pairs={{128,1},{0,129},{130,3},{2,131},{132,5},{4,133},{134,7},{6,135},{1... | collective-permute-start | bytes 1572872 | tf_op jit(solution)/shard_map/ppermute | solution.py:372
  135.9 16.0 %collective-permute-start.17 = (f32[256,512]{1,0:T(8,128)S(1)}, f32[256,512]{1,0:T(8,128)S(1)}, u32[]{:S(2)}, u32[]{:S(2)}) collective-permute-start(f32[256,512]{1,0:T(8,128)S(1)} %get-tuple-element.41.refs_4_), channel_id=1, source_target_pairs={{0,1},{128,129},{2,3},{130,131},{4,5},{132,133},{6,7},{134,135},{8... | collective-permute-start | bytes 1572872 | tf_op jit(solution)/shard_map/ppermute | solution.py:372
  165.6 5.4 %collective-permute-start.19 = (f32[5,128,128]{2,1,0:T(8,128)S(1)}, f32[5,128,128]{2,1,0:T(8,128)S(1)}, u32[]{:S(2)}, u32[]{:S(2)}) collective-permute-start(f32[5,128,128]{2,1,0:T(8,128)S(1)} %bitcast.31), channel_id=1, source_target_pairs={{0,2},{2,0},{1,3},{3,1},{4,6},{6,4},{5,7},{7,5},{8,10},{10,8},{9,1... | collective-permute-start | bytes 983048 | tf_op jit(solution)/shard_map/ppermute | solution.py:363
  165.6 22.9 %collective-permute-start.20 = (f32[256,512]{1,0:T(8,128)S(1)}, f32[256,512]{1,0:T(8,128)S(1)}, u32[]{:S(2)}, u32[]{:S(2)}) collective-permute-start(f32[256,512]{1,0:T(8,128)S(1)} %get-tuple-element.38.refs_0_), channel_id=1, source_target_pairs={{128,0},{129,1},{0,128},{1,129},{130,2},{131,3},{2,130},{3,131},{1... | collective-permute-start | bytes 1572872 | tf_op jit(solution)/shard_map/ppermute | solution.py:372
  167.1 25.6 %collective-permute-start.21 = (f32[256,512]{1,0:T(8,128)S(1)}, f32[256,512]{1,0:T(8,128)S(1)}, u32[]{:S(2)}, u32[]{:S(2)}) collective-permute-start(f32[256,512]{1,0:T(8,128)S(1)} %get-tuple-element.41.refs_4_), channel_id=1, source_target_pairs={{129,1},{1,129},{131,3},{3,131},{133,5},{5,133},{135,7},{7,135},{1... | collective-permute-start | bytes 1572872 | tf_op jit(solution)/shard_map/ppermute | solution.py:372

commit v4 on v3

--- a/solution.py
+++ b/solution.py
@@ -325,8 +325,9 @@
 
 
 def basis_kernel(inverse, *refs):
-    lows, highs = refs[0:4], refs[4:8]
-    out, done, store = refs[8:]
+    lows = [refs[0:1], refs[1:2], refs[2:4], refs[4:5]]
+    highs = refs[5:9]
+    out, done, store = refs[9:]
     here = 2 * lax.axis_index("row") + lax.axis_index("sk")
     chunk, narrow = done.shape[1:]
     form = ((1,), (0,))
@@ -335,8 +336,9 @@
     stores = []
     for n in range(4):
         total = 0.0
-        for (w_high, w_low), part in zip(weights, (lows[n], highs[n])):
-            high, low = split(part[...])
+        parts = (jnp.concatenate([ref[...] for ref in lows[n]], axis=0), highs[n][...])
+        for (w_high, w_low), part in zip(weights, parts):
+            high, low = split(part)
             total += dot(w_high, high, form) + (dot(w_high, low, form) + dot(w_low, high, form))
         done[n] = total.T
         place = pl.ds(pl.multiple_of((here ^ n) * chunk, chunk), chunk)
@@ -350,7 +352,7 @@
     narrow, chunk = lows[0].shape
     return pl.pallas_call(
         basis_kernel,
-        in_specs=[VMEM] * 9,
+        in_specs=[VMEM] * 10,
         out_specs=ANY,
         out_shape=jax.ShapeDtypeStruct((4 * chunk, narrow), F32),
         scratch_shapes=[pltpu.VMEM((4, chunk, narrow), F32), pltpu.SemaphoreType.DMA((4,))],
@@ -417,13 +419,15 @@
     piece = jnp.sum(spread(piece, "z"), axis=0)
     piece, highs[1], highs[3] = lax.optimization_barrier((piece, highs[1], highs[3]))
     own_g = spread(piece, SHEET).reshape(keep.shape)
-    late, latest, _ = lax.optimization_barrier((low, high, own_g))
-    lows[2] = across(late, 2)
-    highs[2] = across(latest, 2, ODD)
+    first, second, late, _ = lax.optimization_barrier((lows[3], lows[1], high, own_g))
+    middle = narrow // 2
+    relayed = [across(first[:middle], 1), across(second[middle:], 3)]
+    lows[2] = None
+    highs[2] = across(late, 2, ODD)
     other_g = swap(own_g)
 
     upper, inverse = cholesky(own_g, other_g, total_rows, width)
-    return basis_of(inverse, lows, highs), upper
+    return basis_of(inverse, lows[:2] + relayed + lows[3:], highs), upper
 
 
 def solution(mesh):

time: 196 us -> 192 us (0.980)
  waiting for transfers between devices: 56.3 us -> 53 us
    ppermute x9 -> x10, waiting for transfers between devices: 31.6 us -> 26.8 us  [across(): return lax.ppermute(x, RING, [(i ^ n, i) for i in to])]
    ppermute x9 -> x10, starting transfers between devices: 15 us -> 15.6 us  [across(): return lax.ppermute(x, RING, [(i ^ n, i) for i in to])]
  transfers between devices with their start and end apart: 22 -> 23, of which waited for: 13 -> 12; matrix products, arithmetic and copies ran while one was open for 0% -> 0% of each run, Pallas kernels for 9% -> 9%
where the time goes in v4:
time: 192 us
  blocking collectives  75.5 us (39%)
  waiting for transfers between devices  53 us (28%)
  Pallas kernels  33.2 us (17%)
  starting transfers between devices  25.7 us (13%)
  local copies, waits for them, and re-layouts  2.63 us (1%)
    all_to_all x5, blocking collectives, exchange(): return lax.all_to_all(x, axes, 0, 0, tiled=True)  75.5 us
    ppermute x10, waiting for transfers between devices, across(): return lax.ppermute(x, RING, [(i ^ n, i) for i in to])  26.8 us
    ppermute x6, waiting for transfers between devices, shift(): return lax.ppermute(x, axes, [(i, (i + n) % size) for i in range(size)])  22.4 us
    pallas_call x1, Pallas kernels, cholesky(): pl.pallas_call(functools.partial(cholesky_kernel, 1.0 / total_rows), out_...  17.5 us
    ppermute x10, starting transfers between devices, across(): return lax.ppermute(x, RING, [(i ^ n, i) for i in to])  15.6 us
    ppermute x6, starting transfers between devices, shift(): return lax.ppermute(x, axes, [(i, (i + n) % size) for i in range(size)])  9.41 us
    pallas_call x1, Pallas kernels, backward(): pl.pallas_call(backward_kernel, in_specs=[SMEM, SMEM, SMEM, ANY] + [VMEM]...  4.68 us
    pallas_call x1, Pallas kernels, forward(): pl.pallas_call(forward_kernel, in_specs=[SMEM, SMEM, SMEM, ANY, VMEM], ou...  4.43 us
  transfers between devices with their start and end apart: 23, of which 12 were waited for; matrix products, arithmetic and copies ran while one was open for 0% of the time, Pallas kernels for 9%

profile of v4, /device:TPU:2, one launch (start us, length us, event | category | flops | bytes accessed | tf_op | source)
XLA Modules:
  0.0 192.0 jit_solution(12438083522706805197)
XLA Ops:
  0.6 0.0 copy-start.4
  0.6 0.0 copy-start.2
  1.3 0.0 copy-start
  1.3 1.2 copy-done
  2.5 0.7 copy-done.1
  3.2 0.7 copy-done.3
  3.9 4.4 %forward.1 = (f32[4,2,256,128]{3,2,1,0:T(8,128)S(1)}, f32[4,2,256,128]{3,2,1,0:T(8,128)S(1)}) custom-call(s32[4]{0:T(128)S(1)} %bitcast.33, s32[4]{0:T(128)S(1)} %bitcast.35, s32[1]{0:T(128)} %bitcast.23.count, bf16[4,1024,1024]{2,1,0:T(8,128)(2,1)} %bitcast.37, bf16[2,1024,256]{2,1,0:T(8,128)(2,1)S(1)} %bitcast.25), custom_call_target="tpu_custom_call" | custom-call | tf_op jit(solution)/shard_map/forward/pallas_call | solution.py:84
  8.3 0.7 collective-permute-start
  8.9 2.3 %collective-permute-done = f32[4,2,256,128]{3,2,1,0:T(8,128)S(1)} collective-permute-done((f32[4,2,256,128]{3,2,1,0:T(8,128)S(1)}, f32[4,2,256,128]{3,2,1,0:T(8,128)S(1)}, u32[]{:S(2)}, u32[]{:S(2)}) %collective-permute-start) | collective-permute-done | bytes 1048608 | tf_op jit(solution)/shard_map/ppermute | solution.py:365
  11.2 0.1 fusion.2
  11.3 1.7 collective-permute-start.1
  13.0 2.9 %collective-permute-start.3 = (f32[2,256,128]{2,1,0:T(8,128)S(1)}, f32[2,256,128]{2,1,0:T(8,128)S(1)}, u32[]{:S(2)}, u32[]{:S(2)}) collective-permute-start(f32[2,256,128]{2,1,0:T(8,128)S(1)} %get-tuple-element.47), channel_id=1, source_target_pairs={{0,8},{4,12},{8,0},{12,4},{1,9},{5,13},{9,1},{13,5},{2,10},{6,14},... | collective-permute-start | bytes 786440 | tf_op jit(solution)/shard_map/ppermute | solution.py:370
  15.9 0.8 collective-permute-start.2
  16.7 4.6 %collective-permute-done.1 = f32[2,256,128]{2,1,0:T(8,128)S(1)} collective-permute-done((f32[2,256,128]{2,1,0:T(8,128)S(1)}, f32[2,256,128]{2,1,0:T(8,128)S(1)}, u32[]{:S(2)}, u32[]{:S(2)}) %collective-permute-start.1) | collective-permute-done | bytes 262176 | tf_op jit(solution)/shard_map/ppermute | solution.py:370
  21.2 6.8 %collective-permute-done.3 = f32[2,256,128]{2,1,0:T(8,128)S(1)} collective-permute-done((f32[2,256,128]{2,1,0:T(8,128)S(1)}, f32[2,256,128]{2,1,0:T(8,128)S(1)}, u32[]{:S(2)}, u32[]{:S(2)}) %collective-permute-start.3) | collective-permute-done | bytes 262176 | tf_op jit(solution)/shard_map/ppermute | solution.py:370
  28.0 0.0 collective-permute-done.2
  28.0 0.1 fusion.6
  28.1 19.5 %all_to_all.25 = f32[8,64,128]{2,1,0:T(8,128)S(1)} all-to-all(f32[8,64,128]{2,1,0:T(8,128)S(1)} %bitcast.40), channel_id=1, replica_groups=mesh['row'=2,'z'=8,'y'=4,'core'=2,'sk'=2] {'z'}, dimensions={0} | all-to-all | bytes 524288 | tf_op jit(solution)/shard_map/all_to_all | solution.py:378
  47.6 12.9 %all_to_all.26 = f32[8,64,128]{2,1,0:T(8,128)S(1)} all-to-all(f32[8,64,128]{2,1,0:T(8,128)S(1)} %broadcast_in_dim.6), channel_id=1, replica_groups=mesh['row'=2,'z'=8,'y'=4,'core'=2,'sk'=2] {'z'}, dimensions={0} | all-to-all | bytes 524288 | tf_op jit(solution)/shard_map/all_to_all | solution.py:378
  60.5 3.1 %collective-permute-start.6 = (f32[2,256,128]{2,1,0:T(8,128)S(1)}, f32[2,256,128]{2,1,0:T(8,128)S(1)}, u32[]{:S(2)}, u32[]{:S(2)}) collective-permute-start(f32[2,256,128]{2,1,0:T(8,128)S(1)} %bitcast.26), channel_id=1, source_target_pairs={{0,12},{4,0},{8,4},{12,8},{1,13},{5,1},{9,5},{13,9},{2,14},{6,2},{... | collective-permute-start | bytes 786440 | tf_op jit(solution)/shard_map/ppermute | solution.py:370
  63.6 0.8 collective-permute-start.5
  64.4 0.2 collective-permute-start.4
  64.6 0.0 collective-permute-start.7
  64.6 7.3 %collective-permute-done.6.rest_3_ = f32[2,256,128]{2,1,0:T(8,128)S(1)} collective-permute-done((f32[2,256,128]{2,1,0:T(8,128)S(1)}, f32[2,256,128]{2,1,0:T(8,128)S(1)}, u32[]{:S(2)}, u32[]{:S(2)}) %collective-permute-start.6) | collective-permute-done | bytes 262176 | tf_op jit(solution)/shard_map/ppermute | solution.py:370
  71.9 0.0 collective-permute-start.10
  72.0 1.0 collective-permute-done.5.rest_2_
  73.0 0.0 collective-permute-start.9
  73.0 2.7 %collective-permute-done.4.rest_1_ = f32[2,256,128]{2,1,0:T(8,128)S(1)} collective-permute-done((f32[2,256,128]{2,1,0:T(8,128)S(1)}, f32[2,256,128]{2,1,0:T(8,128)S(1)}, u32[]{:S(2)}, u32[]{:S(2)}) %collective-permute-start.4) | collective-permute-done | bytes 262176 | tf_op jit(solution)/shard_map/ppermute | solution.py:370
  75.7 0.0 collective-permute-start.8
  75.7 0.0 collective-permute-done.7.rest_4_
  75.7 0.0 collective-permute-done.10.rest_7_
  75.7 0.0 collective-permute-done.9.rest_6_
  75.7 1.5 collective-permute-done.8.rest_5_
  77.2 4.7 %backward.1 = (f32[4,256,128]{2,1,0:T(8,128)S(1)}, f32[4,256,128]{2,1,0:T(8,128)S(1)}, f32[4,256,128]{2,1,0:T(8,128)S(1)}, f32[4,256,128]{2,1,0:T(8,128)S(1)}) custom-call(s32[4]{0:T(128)S(1)} %bitcast.34, s32[4]{0:T(128)S(1)} %bitcast.36, s32[1]{0:T(128)} %bitcast.24.count, bf16[4,1024,1024]{2,1,0:T(8,128)(2,1)} %bitcast.38, f32[2,256,128]{2,1,0:T(8,128)S(1)} %bitcast.30, ...), custom_call_target="tpu_custom_call" | custom-call | tf_op jit(solution)/shard_map/backward/pallas_call | solution.py:132
  81.9 0.6 collective-permute-start.11
  82.5 3.5 %collective-permute-start.12 = (f32[4,256,128]{2,1,0:T(8,128)S(1)}, f32[4,256,128]{2,1,0:T(8,128)S(1)}, u32[]{:S(2)}, u32[]{:S(2)}) collective-permute-start(f32[4,256,128]{2,1,0:T(8,128)S(1)} %get-tuple-element.28), channel_id=1, source_target_pairs={{128,0},{129,1},{0,128},{1,129},{130,2},{131,3},{2,130},{3,131},{1... | collective-permute-start | bytes 1572872 | tf_op jit(solution)/shard_map/ppermute | solution.py:374
  86.0 0.0 collective-permute-start.13
  86.0 10.8 %collective-permute-done.11.refs_1_ = f32[4,256,128]{2,1,0:T(8,128)S(1)} collective-permute-done((f32[4,256,128]{2,1,0:T(8,128)S(1)}, f32[4,256,128]{2,1,0:T(8,128)S(1)}, u32[]{:S(2)}, u32[]{:S(2)}) %collective-permute-start.11) | collective-permute-done | bytes 524320 | tf_op jit(solution)/shard_map/ppermute | solution.py:374
  96.8 12.5 %collective-permute-done.12.refs_2_ = f32[4,256,128]{2,1,0:T(8,128)S(1)} collective-permute-done((f32[4,256,128]{2,1,0:T(8,128)S(1)}, f32[4,256,128]{2,1,0:T(8,128)S(1)}, u32[]{:S(2)}, u32[]{:S(2)}) %collective-permute-start.12) | collective-permute-done | bytes 524320 | tf_op jit(solution)/shard_map/ppermute | solution.py:374
  109.2 1.4 collective-permute-done.13.refs_3_
  110.6 3.8 %gram.1 = (f32[256,512]{1,0:T(8,128)S(1)}, f32[256,512]{1,0:T(8,128)S(1)}, f32[5,128,128]{2,1,0:T(8,128)S(1)}, f32[5,128,128]{2,1,0:T(8,128)S(1)}) custom-call(f32[4,256,128]{2,1,0:T(8,128)S(1)} %get-tuple-element.26.refs_0_, f32[4,256,128]{2,1,0:T(8,128)S(1)} %collective-permute-done.11.refs_1_, f32[4,256,128]{2,1,0:T(8,128)S(1)} %collective-permute-done.12.refs_2_, ...), custom_call_target="tpu_custom_call" | custom-call | tf_op jit(solution)/shard_map/gram/pallas_call | solution.py:189
  114.4 0.1 collective-permute-start.14
  114.5 0.4 collective-permute-start.16
  114.8 3.0 %collective-permute-start.15 = (f32[256,512]{1,0:T(8,128)S(1)}, f32[256,512]{1,0:T(8,128)S(1)}, u32[]{:S(2)}, u32[]{:S(2)}) collective-permute-start(f32[256,512]{1,0:T(8,128)S(1)} %get-tuple-element.32.refs_0_), channel_id=1, source_target_pairs={{1,0},{0,1},{129,128},{128,129},{3,2},{2,3},{131,130},{130,131},{5... | collective-permute-start | bytes 1572872 | tf_op jit(solution)/shard_map/ppermute | solution.py:374
  117.9 0.0 collective-permute-done.14
  117.9 17.7 %all_to_all.27 = f32[16,40,128]{2,1,0:T(8,128)S(1)} all-to-all(f32[16,40,128]{2,1,0:T(8,128)S(1)} %bitcast.39), channel_id=1, replica_groups=mesh['row'=2,'z'=8,'y'=4,'core'=2,'sk'=2] {'row','y','sk'}, dimensions={0} | all-to-all | bytes 655360 | tf_op jit(solution)/shard_map/all_to_all | solution.py:378
  135.6 0.0 collective-permute-done.16.refs_4_
  135.6 0.0 collective-permute-done.15.refs_1_
  135.6 1.3 collective-permute-start.18
  136.9 1.3 collective-permute-start.17
  138.2 11.9 %all_to_all.28 = f32[8,40,128]{2,1,0:T(8,128)S(1)} all-to-all(f32[8,40,128]{2,1,0:T(8,128)S(1)} %broadcast_in_dim.7), channel_id=1, replica_groups=mesh['row'=2,'z'=8,'y'=4,'core'=2,'sk'=2] {'z'}, dimensions={0} | all-to-all | bytes 327680 | tf_op jit(solution)/shard_map/all_to_all | solution.py:378
  150.2 0.5 collective-permute-done.18.refs_8_
  150.7 1.7 collective-permute-done.17.refs_6_
  152.4 13.5 %all_to_all.29 = f32[16,40,128]{2,1,0:T(8,128)S(1)} all-to-all(f32[16,40,128]{2,1,0:T(8,128)S(1)} %broadcast_in_dim.8), channel_id=1, replica_groups=mesh['row'=2,'z'=8,'y'=4,'core'=2,'sk'=2] {'row','y','sk'}, dimensions={0} | all-to-all | bytes 655360 | tf_op jit(solution)/shard_map/all_to_all | solution.py:378
  165.9 0.0 collective-permute-start.19
  166.0 0.7 collective-permute-start.21
  166.7 2.0 %collective-permute-start.20 = (f32[128,512]{1,0:T(8,128)S(1)}, f32[128,512]{1,0:T(8,128)S(1)}, u32[]{:S(2)}, u32[]{:S(2)}) collective-permute-start(f32[128,512]{1,0:T(8,128)S(1)} %slice.38), channel_id=1, source_target_pairs={{1,0},{0,1},{129,128},{128,129},{3,2},{2,3},{131,130},{130,131},{5... | collective-permute-start | bytes 786440 | tf_op jit(solution)/shard_map/ppermute | solution.py:374
  168.7 2.8 %collective-permute-start.22 = (f32[256,512]{1,0:T(8,128)S(1)}, f32[256,512]{1,0:T(8,128)S(1)}, u32[]{:S(2)}, u32[]{:S(2)}) collective-permute-start(f32[256,512]{1,0:T(8,128)S(1)} %get-tuple-element.43.refs_5_), channel_id=1, source_target_pairs={{129,1},{1,129},{131,3},{3,131},{133,5},{5,133},{135,7},{7,135},{1... | collective-permute-start | bytes 1572872 | tf_op jit(solution)/shard_map/ppermute | solution.py:374
  171.5 0.0 collective-permute-done.19.other
  171.5 17.5 %cholesky.1 = (f32[512,512]{1,0:T(8,128)}, f32[512,512]{1,0:T(8,128)S(1)}) custom-call(f32[5,128,128]{2,1,0:T(8,128)S(1)} %bitcast.32, f32[5,128,128]{2,1,0:T(8,128)S(1)} %collective-permute-done.19.other), custom_call_target="tpu_custom_call" | custom-call | flops 17179869184 | bytes 4194304 | tf_op jit(solution)/shard_map/cholesky/pallas_call | solution.py:312
  189.0 0.0 collective-permute-done.21.refs_3_
  189.0 0.0 collective-permute-done.20.refs_2_
  189.0 0.0 collective-permute-done.22.refs_7_
  189.0 2.8 %basis.1 = f32[2048,256]{1,0:T(8,128)} custom-call(f32[512,512]{1,0:T(8,128)S(1)} %get-tuple-element.37.inverse, f32[256,512]{1,0:T(8,128)S(1)} %get-tuple-element.32.refs_0_, f32[256,512]{1,0:T(8,128)S(1)} %collective-permute-done.15.refs_1_, f32[128,512]{1,0:T(8,128)S(1)} %collective-permute-done.20.refs_2_, ...), custom_call_target="tpu_custom_call" | custom-call | tf_op jit(solution)/shard_map/basis/pallas_call | solution.py:353
  (14 shorter events, 0.2 us)
Async XLA Ops:
  0.6 76.6 %copy-start.4 = (s32[1,1,4]{2,1,0:T(1,128)S(1)}, s32[1,1,4]{2,1,0:T(1,128)}, u32[]{:S(2)}) copy-start(s32[1,1,4]{2,1,0:T(1,128)} %param.7) | copy-start | bytes 52
  0.6 76.6 %copy-start.2 = (s32[1,1,4]{2,1,0:T(1,128)S(1)}, s32[1,1,4]{2,1,0:T(1,128)}, u32[]{:S(2)}) copy-start(s32[1,1,4]{2,1,0:T(1,128)} %param.6) | copy-start | bytes 52
  1.3 1.2 copy-start
  2.5 0.7 copy-start.1
  3.2 0.7 copy-start.3
  8.3 2.9 %collective-permute-start = (f32[4,2,256,128]{3,2,1,0:T(8,128)S(1)}, f32[4,2,256,128]{3,2,1,0:T(8,128)S(1)}, u32[]{:S(2)}, u32[]{:S(2)}) collective-permute-start(f32[4,2,256,128]{3,2,1,0:T(8,128)S(1)} %get-tuple-element.25), channel_id=1, source_target_pairs={{0,2},{2,0},{1,3},{3,1},{4,6},{6,4},{5,7},{7,5},{8,10},{10,8},{9,1... | collective-permute-start | bytes 3145736 | tf_op jit(solution)/shard_map/ppermute | solution.py:365
  11.3 9.9 %collective-permute-start.1 = (f32[2,256,128]{2,1,0:T(8,128)S(1)}, f32[2,256,128]{2,1,0:T(8,128)S(1)}, u32[]{:S(2)}, u32[]{:S(2)}) collective-permute-start(f32[2,256,128]{2,1,0:T(8,128)S(1)} %get-tuple-element.46), channel_id=1, source_target_pairs={{0,4},{4,8},{8,12},{12,0},{1,5},{5,9},{9,13},{13,1},{2,6},{6,10},{... | collective-permute-start | bytes 786440 | tf_op jit(solution)/shard_map/ppermute | solution.py:370
  13.0 15.1 %collective-permute-start.3 = (f32[2,256,128]{2,1,0:T(8,128)S(1)}, f32[2,256,128]{2,1,0:T(8,128)S(1)}, u32[]{:S(2)}, u32[]{:S(2)}) collective-permute-start(f32[2,256,128]{2,1,0:T(8,128)S(1)} %get-tuple-element.47), channel_id=1, source_target_pairs={{0,8},{4,12},{8,0},{12,4},{1,9},{5,13},{9,1},{13,5},{2,10},{6,14},... | collective-permute-start | bytes 786440 | tf_op jit(solution)/shard_map/ppermute | solution.py:370
  15.9 12.2 %collective-permute-start.2 = (f32[2,256,128]{2,1,0:T(8,128)S(1)}, f32[2,256,128]{2,1,0:T(8,128)S(1)}, u32[]{:S(2)}, u32[]{:S(2)}) collective-permute-start(f32[2,256,128]{2,1,0:T(8,128)S(1)} %get-tuple-element.48), channel_id=1, source_target_pairs={{0,12},{4,0},{8,4},{12,8},{1,13},{5,1},{9,5},{13,9},{2,14},{6,2},{... | collective-permute-start | bytes 786440 | tf_op jit(solution)/shard_map/ppermute | solution.py:370
  60.5 11.4 %collective-permute-start.6 = (f32[2,256,128]{2,1,0:T(8,128)S(1)}, f32[2,256,128]{2,1,0:T(8,128)S(1)}, u32[]{:S(2)}, u32[]{:S(2)}) collective-permute-start(f32[2,256,128]{2,1,0:T(8,128)S(1)} %bitcast.26), channel_id=1, source_target_pairs={{0,12},{4,0},{8,4},{12,8},{1,13},{5,1},{9,5},{13,9},{2,14},{6,2},{... | collective-permute-start | bytes 786440 | tf_op jit(solution)/shard_map/ppermute | solution.py:370
  63.6 9.4 %collective-permute-start.5 = (f32[2,256,128]{2,1,0:T(8,128)S(1)}, f32[2,256,128]{2,1,0:T(8,128)S(1)}, u32[]{:S(2)}, u32[]{:S(2)}) collective-permute-start(f32[2,256,128]{2,1,0:T(8,128)S(1)} %bitcast.27), channel_id=1, source_target_pairs={{0,8},{4,12},{8,0},{12,4},{1,9},{5,13},{9,1},{13,5},{2,10},{6,14},... | collective-permute-start | bytes 786440 | tf_op jit(solution)/shard_map/ppermute | solution.py:370
  64.4 11.2 %collective-permute-start.4 = (f32[2,256,128]{2,1,0:T(8,128)S(1)}, f32[2,256,128]{2,1,0:T(8,128)S(1)}, u32[]{:S(2)}, u32[]{:S(2)}) collective-permute-start(f32[2,256,128]{2,1,0:T(8,128)S(1)} %bitcast.28), channel_id=1, source_target_pairs={{0,4},{4,8},{8,12},{12,0},{1,5},{5,9},{9,13},{13,1},{2,6},{6,10},{... | collective-permute-start | bytes 786440 | tf_op jit(solution)/shard_map/ppermute | solution.py:370
  64.6 11.1 %collective-permute-start.7 = (f32[2,256,128]{2,1,0:T(8,128)S(1)}, f32[2,256,128]{2,1,0:T(8,128)S(1)}, u32[]{:S(2)}, u32[]{:S(2)}) collective-permute-start(f32[2,256,128]{2,1,0:T(8,128)S(1)} %bitcast.29), channel_id=1, source_target_pairs={{0,2},{2,0},{1,3},{3,1},{4,6},{6,4},{5,7},{7,5},{8,10},{10,8},{9,1... | collective-permute-start | bytes 786440 | tf_op jit(solution)/shard_map/ppermute | solution.py:365
  71.9 3.7 %collective-permute-start.10 = (f32[2,256,128]{2,1,0:T(8,128)S(1)}, f32[2,256,128]{2,1,0:T(8,128)S(1)}, u32[]{:S(2)}, u32[]{:S(2)}) collective-permute-start(f32[2,256,128]{2,1,0:T(8,128)S(1)} %collective-permute-done.6.rest_3_), channel_id=1, source_target_pairs={{0,2},{2,0},{1,3},{3,1},{4,6},{6,4},{5,7},{7,5},{8,10},{10,8},{9,1... | collective-permute-start | bytes 786440 | tf_op jit(solution)/shard_map/ppermute | solution.py:365
  73.0 2.7 %collective-permute-start.9 = (f32[2,256,128]{2,1,0:T(8,128)S(1)}, f32[2,256,128]{2,1,0:T(8,128)S(1)}, u32[]{:S(2)}, u32[]{:S(2)}) collective-permute-start(f32[2,256,128]{2,1,0:T(8,128)S(1)} %collective-permute-done.5.rest_2_), channel_id=1, source_target_pairs={{0,2},{2,0},{1,3},{3,1},{4,6},{6,4},{5,7},{7,5},{8,10},{10,8},{9,1... | collective-permute-start | bytes 786440 | tf_op jit(solution)/shard_map/ppermute | solution.py:365
  75.7 1.5 collective-permute-start.8
  81.9 14.9 %collective-permute-start.11 = (f32[4,256,128]{2,1,0:T(8,128)S(1)}, f32[4,256,128]{2,1,0:T(8,128)S(1)}, u32[]{:S(2)}, u32[]{:S(2)}) collective-permute-start(f32[4,256,128]{2,1,0:T(8,128)S(1)} %get-tuple-element.27), channel_id=1, source_target_pairs={{1,0},{0,1},{129,128},{128,129},{3,2},{2,3},{131,130},{130,131},{5... | collective-permute-start | bytes 1572872 | tf_op jit(solution)/shard_map/ppermute | solution.py:374
  82.5 26.7 %collective-permute-start.12 = (f32[4,256,128]{2,1,0:T(8,128)S(1)}, f32[4,256,128]{2,1,0:T(8,128)S(1)}, u32[]{:S(2)}, u32[]{:S(2)}) collective-permute-start(f32[4,256,128]{2,1,0:T(8,128)S(1)} %get-tuple-element.28), channel_id=1, source_target_pairs={{128,0},{129,1},{0,128},{1,129},{130,2},{131,3},{2,130},{3,131},{1... | collective-permute-start | bytes 1572872 | tf_op jit(solution)/shard_map/ppermute | solution.py:374
  86.0 24.6 %collective-permute-start.13 = (f32[4,256,128]{2,1,0:T(8,128)S(1)}, f32[4,256,128]{2,1,0:T(8,128)S(1)}, u32[]{:S(2)}, u32[]{:S(2)}) collective-permute-start(f32[4,256,128]{2,1,0:T(8,128)S(1)} %get-tuple-element.29), channel_id=1, source_target_pairs={{129,0},{128,1},{1,128},{0,129},{131,2},{130,3},{3,130},{2,131},{1... | collective-permute-start | bytes 1572872 | tf_op jit(solution)/shard_map/ppermute | solution.py:374
  114.4 3.5 %collective-permute-start.14 = (f32[5,128,128]{2,1,0:T(8,128)S(1)}, f32[5,128,128]{2,1,0:T(8,128)S(1)}, u32[]{:S(2)}, u32[]{:S(2)}) collective-permute-start(f32[5,128,128]{2,1,0:T(8,128)S(1)} %get-tuple-element.31), channel_id=1, source_target_pairs={{0,2},{2,0},{1,3},{3,1},{4,6},{6,4},{5,7},{7,5},{8,10},{10,8},{9,1... | collective-permute-start | bytes 983048 | tf_op jit(solution)/shard_map/ppermute | solution.py:365
  114.5 21.1 %collective-permute-start.16 = (f32[256,512]{1,0:T(8,128)S(1)}, f32[256,512]{1,0:T(8,128)S(1)}, u32[]{:S(2)}, u32[]{:S(2)}) collective-permute-start(f32[256,512]{1,0:T(8,128)S(1)} %get-tuple-element.32.refs_0_), channel_id=1, source_target_pairs={{129,0},{128,1},{1,128},{0,129},{131,2},{130,3},{3,130},{2,131},{1... | collective-permute-start | bytes 1572872 | tf_op jit(solution)/shard_map/ppermute | solution.py:374
  114.8 20.8 %collective-permute-start.15 = (f32[256,512]{1,0:T(8,128)S(1)}, f32[256,512]{1,0:T(8,128)S(1)}, u32[]{:S(2)}, u32[]{:S(2)}) collective-permute-start(f32[256,512]{1,0:T(8,128)S(1)} %get-tuple-element.32.refs_0_), channel_id=1, source_target_pairs={{1,0},{0,1},{129,128},{128,129},{3,2},{2,3},{131,130},{130,131},{5... | collective-permute-start | bytes 1572872 | tf_op jit(solution)/shard_map/ppermute | solution.py:374
  135.6 15.1 %collective-permute-start.18 = (f32[256,512]{1,0:T(8,128)S(1)}, f32[256,512]{1,0:T(8,128)S(1)}, u32[]{:S(2)}, u32[]{:S(2)}) collective-permute-start(f32[256,512]{1,0:T(8,128)S(1)} %get-tuple-element.43.refs_5_), channel_id=1, source_target_pairs={{128,1},{0,129},{130,3},{2,131},{132,5},{4,133},{134,7},{6,135},{1... | collective-permute-start | bytes 1572872 | tf_op jit(solution)/shard_map/ppermute | solution.py:374
  136.9 15.4 %collective-permute-start.17 = (f32[256,512]{1,0:T(8,128)S(1)}, f32[256,512]{1,0:T(8,128)S(1)}, u32[]{:S(2)}, u32[]{:S(2)}) collective-permute-start(f32[256,512]{1,0:T(8,128)S(1)} %get-tuple-element.43.refs_5_), channel_id=1, source_target_pairs={{0,1},{128,129},{2,3},{130,131},{4,5},{132,133},{6,7},{134,135},{8... | collective-permute-start | bytes 1572872 | tf_op jit(solution)/shard_map/ppermute | solution.py:374
  165.9 5.6 %collective-permute-start.19 = (f32[5,128,128]{2,1,0:T(8,128)S(1)}, f32[5,128,128]{2,1,0:T(8,128)S(1)}, u32[]{:S(2)}, u32[]{:S(2)}) collective-permute-start(f32[5,128,128]{2,1,0:T(8,128)S(1)} %bitcast.31), channel_id=1, source_target_pairs={{0,2},{2,0},{1,3},{3,1},{4,6},{6,4},{5,7},{7,5},{8,10},{10,8},{9,1... | collective-permute-start | bytes 983048 | tf_op jit(solution)/shard_map/ppermute | solution.py:365
  166.0 23.0 %collective-permute-start.21 = (f32[128,512]{1,0:T(8,128)S(1)}, f32[128,512]{1,0:T(8,128)S(1)}, u32[]{:S(2)}, u32[]{:S(2)}) collective-permute-start(f32[128,512]{1,0:T(8,128)S(1)} %slice.39), channel_id=1, source_target_pairs={{129,0},{128,1},{1,128},{0,129},{131,2},{130,3},{3,130},{2,131},{1... | collective-permute-start | bytes 786440 | tf_op jit(solution)/shard_map/ppermute | solution.py:374
  166.7 22.3 %collective-permute-start.20 = (f32[128,512]{1,0:T(8,128)S(1)}, f32[128,512]{1,0:T(8,128)S(1)}, u32[]{:S(2)}, u32[]{:S(2)}) collective-permute-start(f32[128,512]{1,0:T(8,128)S(1)} %slice.38), channel_id=1, source_target_pairs={{1,0},{0,1},{129,128},{128,129},{3,2},{2,3},{131,130},{130,131},{5... | collective-permute-start | bytes 786440 | tf_op jit(solution)/shard_map/ppermute | solution.py:374
  168.7 20.3 %collective-permute-start.22 = (f32[256,512]{1,0:T(8,128)S(1)}, f32[256,512]{1,0:T(8,128)S(1)}, u32[]{:S(2)}, u32[]{:S(2)}) collective-permute-start(f32[256,512]{1,0:T(8,128)S(1)} %get-tuple-element.43.refs_5_), channel_id=1, source_target_pairs={{129,1},{1,129},{131,3},{3,131},{133,5},{5,133},{135,7},{7,135},{1... | collective-permute-start | bytes 1572872 | tf_op jit(solution)/shard_map/ppermute | solution.py:374

commit v5 on v4

--- a/solution.py
+++ b/solution.py
@@ -278,8 +278,9 @@
             eliminate(d, base)
             if base + SUB < SIDE:
                 panel = d[base : base + SUB, :]
-                left = panel[:, base + SUB : SIDE]
-                d[base + SUB :, :] -= dot(left, panel, ((0,), (0,)), HIGH)
+                for r in (slice(base + SUB, base + 2 * SUB), slice(base + 2 * SUB, SIDE)):
+                    if r.start < r.stop:
+                        d[r, :] -= dot(panel[:, r], panel, ((0,), (0,)), HIGH)
         upper[here, here] = jnp.where(row <= col, d[:, 0:SIDE], 0.0)
         inverse[here, here] = jnp.where(row >= col, d[:, SIDE:], 0.0)
 

time: 192 us -> 192 us (level)
  transfers between devices with their start and end apart: 23 -> 23, of which waited for: 12 -> 11; matrix products, arithmetic and copies ran while one was open for 0% -> 0% of each run, Pallas kernels for 9% -> 9%
where the time goes in v5:
time: 192 us; the launch traced here: 191 us
  blocking collectives  76.9 us (40%)
  waiting for transfers between devices  51.1 us (27%)
  Pallas kernels  32.7 us (17%)
  starting transfers between devices  25.9 us (13%)
  local copies, waits for them, and re-layouts  2.63 us (1%)
    all_to_all x5, blocking collectives, exchange(): return lax.all_to_all(x, axes, 0, 0, tiled=True)  76.9 us
    ppermute x10, waiting for transfers between devices, across(): return lax.ppermute(x, RING, [(i ^ n, i) for i in to])  25.9 us
    ppermute x6, waiting for transfers between devices, shift(): return lax.ppermute(x, axes, [(i, (i + n) % size) for i in range(size)])  21 us
    pallas_call x1, Pallas kernels, cholesky(): pl.pallas_call(functools.partial(cholesky_kernel, 1.0 / total_rows), out_...  17 us
    ppermute x10, starting transfers between devices, across(): return lax.ppermute(x, RING, [(i ^ n, i) for i in to])  15.4 us
    ppermute x6, starting transfers between devices, shift(): return lax.ppermute(x, axes, [(i, (i + n) % size) for i in range(size)])  10.3 us
    pallas_call x1, Pallas kernels, backward(): pl.pallas_call(backward_kernel, in_specs=[SMEM, SMEM, SMEM, ANY] + [VMEM]...  4.68 us
    pallas_call x1, Pallas kernels, forward(): pl.pallas_call(forward_kernel, in_specs=[SMEM, SMEM, SMEM, ANY, VMEM], ou...  4.43 us
  transfers between devices with their start and end apart: 23, of which 11 were waited for; matrix products, arithmetic and copies ran while one was open for 0% of the time, Pallas kernels for 9%

profile of v5, /device:TPU:2, one launch (start us, length us, event | category | flops | bytes accessed | tf_op | source)
XLA Modules:
  0.0 191.1 jit_solution(14796549577719985026)
XLA Ops:
  0.6 0.0 copy-start.4
  0.6 0.0 copy-start.2
  1.3 0.0 copy-start
  1.3 1.2 copy-done
  2.5 0.7 copy-done.1
  3.2 0.7 copy-done.3
  3.9 4.4 %forward.1 = (f32[4,2,256,128]{3,2,1,0:T(8,128)S(1)}, f32[4,2,256,128]{3,2,1,0:T(8,128)S(1)}) custom-call(s32[4]{0:T(128)S(1)} %bitcast.33, s32[4]{0:T(128)S(1)} %bitcast.35, s32[1]{0:T(128)} %bitcast.23.count, bf16[4,1024,1024]{2,1,0:T(8,128)(2,1)} %bitcast.37, bf16[2,1024,256]{2,1,0:T(8,128)(2,1)S(1)} %bitcast.25), custom_call_target="tpu_custom_call" | custom-call | tf_op jit(solution)/shard_map/forward/pallas_call | solution.py:84
  8.3 0.1 collective-permute-start
  8.4 2.6 %collective-permute-done = f32[4,2,256,128]{3,2,1,0:T(8,128)S(1)} collective-permute-done((f32[4,2,256,128]{3,2,1,0:T(8,128)S(1)}, f32[4,2,256,128]{3,2,1,0:T(8,128)S(1)}, u32[]{:S(2)}, u32[]{:S(2)}) %collective-permute-start) | collective-permute-done | bytes 1048608 | tf_op jit(solution)/shard_map/ppermute | solution.py:366
  11.0 0.1 fusion.2
  11.1 1.7 collective-permute-start.1
  12.8 2.5 %collective-permute-start.3 = (f32[2,256,128]{2,1,0:T(8,128)S(1)}, f32[2,256,128]{2,1,0:T(8,128)S(1)}, u32[]{:S(2)}, u32[]{:S(2)}) collective-permute-start(f32[2,256,128]{2,1,0:T(8,128)S(1)} %get-tuple-element.47), channel_id=1, source_target_pairs={{0,8},{4,12},{8,0},{12,4},{1,9},{5,13},{9,1},{13,5},{2,10},{6,14},... | collective-permute-start | bytes 786440 | tf_op jit(solution)/shard_map/ppermute | solution.py:371
  15.3 1.3 collective-permute-start.2
  16.7 4.1 %collective-permute-done.1 = f32[2,256,128]{2,1,0:T(8,128)S(1)} collective-permute-done((f32[2,256,128]{2,1,0:T(8,128)S(1)}, f32[2,256,128]{2,1,0:T(8,128)S(1)}, u32[]{:S(2)}, u32[]{:S(2)}) %collective-permute-start.1) | collective-permute-done | bytes 262176 | tf_op jit(solution)/shard_map/ppermute | solution.py:371
  20.8 6.6 %collective-permute-done.3 = f32[2,256,128]{2,1,0:T(8,128)S(1)} collective-permute-done((f32[2,256,128]{2,1,0:T(8,128)S(1)}, f32[2,256,128]{2,1,0:T(8,128)S(1)}, u32[]{:S(2)}, u32[]{:S(2)}) %collective-permute-start.3) | collective-permute-done | bytes 262176 | tf_op jit(solution)/shard_map/ppermute | solution.py:371
  27.3 0.0 collective-permute-done.2
  27.3 0.1 fusion.6
  27.4 19.5 %all_to_all.25 = f32[8,64,128]{2,1,0:T(8,128)S(1)} all-to-all(f32[8,64,128]{2,1,0:T(8,128)S(1)} %bitcast.40), channel_id=1, replica_groups=mesh['row'=2,'z'=8,'y'=4,'core'=2,'sk'=2] {'z'}, dimensions={0} | all-to-all | bytes 524288 | tf_op jit(solution)/shard_map/all_to_all | solution.py:379
  47.0 12.9 %all_to_all.26 = f32[8,64,128]{2,1,0:T(8,128)S(1)} all-to-all(f32[8,64,128]{2,1,0:T(8,128)S(1)} %broadcast_in_dim.6), channel_id=1, replica_groups=mesh['row'=2,'z'=8,'y'=4,'core'=2,'sk'=2] {'z'}, dimensions={0} | all-to-all | bytes 524288 | tf_op jit(solution)/shard_map/all_to_all | solution.py:379
  59.9 3.3 %collective-permute-start.6 = (f32[2,256,128]{2,1,0:T(8,128)S(1)}, f32[2,256,128]{2,1,0:T(8,128)S(1)}, u32[]{:S(2)}, u32[]{:S(2)}) collective-permute-start(f32[2,256,128]{2,1,0:T(8,128)S(1)} %bitcast.26), channel_id=1, source_target_pairs={{0,12},{4,0},{8,4},{12,8},{1,13},{5,1},{9,5},{13,9},{2,14},{6,2},{... | collective-permute-start | bytes 786440 | tf_op jit(solution)/shard_map/ppermute | solution.py:371
  63.2 0.0 collective-permute-start.5
  63.2 1.4 collective-permute-start.4
  64.6 0.0 collective-permute-start.7
  64.6 6.9 %collective-permute-done.6.rest_3_ = f32[2,256,128]{2,1,0:T(8,128)S(1)} collective-permute-done((f32[2,256,128]{2,1,0:T(8,128)S(1)}, f32[2,256,128]{2,1,0:T(8,128)S(1)}, u32[]{:S(2)}, u32[]{:S(2)}) %collective-permute-start.6) | collective-permute-done | bytes 262176 | tf_op jit(solution)/shard_map/ppermute | solution.py:371
  71.5 0.0 collective-permute-start.10
  71.5 1.0 collective-permute-done.5.rest_2_
  72.6 0.0 collective-permute-start.9
  72.6 2.4 %collective-permute-done.4.rest_1_ = f32[2,256,128]{2,1,0:T(8,128)S(1)} collective-permute-done((f32[2,256,128]{2,1,0:T(8,128)S(1)}, f32[2,256,128]{2,1,0:T(8,128)S(1)}, u32[]{:S(2)}, u32[]{:S(2)}) %collective-permute-start.4) | collective-permute-done | bytes 262176 | tf_op jit(solution)/shard_map/ppermute | solution.py:371
  74.9 0.0 collective-permute-start.8
  74.9 0.0 collective-permute-done.7.rest_4_
  74.9 0.0 collective-permute-done.10.rest_7_
  74.9 0.0 collective-permute-done.9.rest_6_
  75.0 1.5 collective-permute-done.8.rest_5_
  76.5 4.7 %backward.1 = (f32[4,256,128]{2,1,0:T(8,128)S(1)}, f32[4,256,128]{2,1,0:T(8,128)S(1)}, f32[4,256,128]{2,1,0:T(8,128)S(1)}, f32[4,256,128]{2,1,0:T(8,128)S(1)}) custom-call(s32[4]{0:T(128)S(1)} %bitcast.34, s32[4]{0:T(128)S(1)} %bitcast.36, s32[1]{0:T(128)} %bitcast.24.count, bf16[4,1024,1024]{2,1,0:T(8,128)(2,1)} %bitcast.38, f32[2,256,128]{2,1,0:T(8,128)S(1)} %bitcast.30, ...), custom_call_target="tpu_custom_call" | custom-call | tf_op jit(solution)/shard_map/backward/pallas_call | solution.py:132
  81.2 0.6 collective-permute-start.11
  81.8 3.3 %collective-permute-start.12 = (f32[4,256,128]{2,1,0:T(8,128)S(1)}, f32[4,256,128]{2,1,0:T(8,128)S(1)}, u32[]{:S(2)}, u32[]{:S(2)}) collective-permute-start(f32[4,256,128]{2,1,0:T(8,128)S(1)} %get-tuple-element.28), channel_id=1, source_target_pairs={{128,0},{129,1},{0,128},{1,129},{130,2},{131,3},{2,130},{3,131},{1... | collective-permute-start | bytes 1572872 | tf_op jit(solution)/shard_map/ppermute | solution.py:375
  85.1 0.0 collective-permute-start.13
  85.1 10.9 %collective-permute-done.11.refs_1_ = f32[4,256,128]{2,1,0:T(8,128)S(1)} collective-permute-done((f32[4,256,128]{2,1,0:T(8,128)S(1)}, f32[4,256,128]{2,1,0:T(8,128)S(1)}, u32[]{:S(2)}, u32[]{:S(2)}) %collective-permute-start.11) | collective-permute-done | bytes 524320 | tf_op jit(solution)/shard_map/ppermute | solution.py:375
  96.0 11.9 %collective-permute-done.12.refs_2_ = f32[4,256,128]{2,1,0:T(8,128)S(1)} collective-permute-done((f32[4,256,128]{2,1,0:T(8,128)S(1)}, f32[4,256,128]{2,1,0:T(8,128)S(1)}, u32[]{:S(2)}, u32[]{:S(2)}) %collective-permute-start.12) | collective-permute-done | bytes 524320 | tf_op jit(solution)/shard_map/ppermute | solution.py:375
  108.0 1.4 collective-permute-done.13.refs_3_
  109.3 3.8 %gram.1 = (f32[256,512]{1,0:T(8,128)S(1)}, f32[256,512]{1,0:T(8,128)S(1)}, f32[5,128,128]{2,1,0:T(8,128)S(1)}, f32[5,128,128]{2,1,0:T(8,128)S(1)}) custom-call(f32[4,256,128]{2,1,0:T(8,128)S(1)} %get-tuple-element.26.refs_0_, f32[4,256,128]{2,1,0:T(8,128)S(1)} %collective-permute-done.11.refs_1_, f32[4,256,128]{2,1,0:T(8,128)S(1)} %collective-permute-done.12.refs_2_, ...), custom_call_target="tpu_custom_call" | custom-call | tf_op jit(solution)/shard_map/gram/pallas_call | solution.py:189
  113.1 0.1 collective-permute-start.14
  113.2 0.4 collective-permute-start.16
  113.6 3.0 %collective-permute-start.15 = (f32[256,512]{1,0:T(8,128)S(1)}, f32[256,512]{1,0:T(8,128)S(1)}, u32[]{:S(2)}, u32[]{:S(2)}) collective-permute-start(f32[256,512]{1,0:T(8,128)S(1)} %get-tuple-element.32.refs_0_), channel_id=1, source_target_pairs={{1,0},{0,1},{129,128},{128,129},{3,2},{2,3},{131,130},{130,131},{5... | collective-permute-start | bytes 1572872 | tf_op jit(solution)/shard_map/ppermute | solution.py:375
  116.6 0.0 collective-permute-done.14
  116.6 17.9 %all_to_all.27 = f32[16,40,128]{2,1,0:T(8,128)S(1)} all-to-all(f32[16,40,128]{2,1,0:T(8,128)S(1)} %bitcast.39), channel_id=1, replica_groups=mesh['row'=2,'z'=8,'y'=4,'core'=2,'sk'=2] {'row','y','sk'}, dimensions={0} | all-to-all | bytes 655360 | tf_op jit(solution)/shard_map/all_to_all | solution.py:379
  134.6 0.0 collective-permute-done.16.refs_4_
  134.6 0.0 collective-permute-done.15.refs_1_
  134.6 1.3 collective-permute-start.18
  135.9 1.3 collective-permute-start.17
  137.2 13.2 %all_to_all.28 = f32[8,40,128]{2,1,0:T(8,128)S(1)} all-to-all(f32[8,40,128]{2,1,0:T(8,128)S(1)} %broadcast_in_dim.7), channel_id=1, replica_groups=mesh['row'=2,'z'=8,'y'=4,'core'=2,'sk'=2] {'z'}, dimensions={0} | all-to-all | bytes 327680 | tf_op jit(solution)/shard_map/all_to_all | solution.py:379
  150.4 0.0 collective-permute-done.18.refs_8_
  150.4 1.7 collective-permute-done.17.refs_6_
  152.2 13.3 %all_to_all.29 = f32[16,40,128]{2,1,0:T(8,128)S(1)} all-to-all(f32[16,40,128]{2,1,0:T(8,128)S(1)} %broadcast_in_dim.8), channel_id=1, replica_groups=mesh['row'=2,'z'=8,'y'=4,'core'=2,'sk'=2] {'row','y','sk'}, dimensions={0} | all-to-all | bytes 655360 | tf_op jit(solution)/shard_map/all_to_all | solution.py:379
  165.5 0.0 collective-permute-start.19
  165.5 0.7 collective-permute-start.21
  166.3 2.0 %collective-permute-start.20 = (f32[128,512]{1,0:T(8,128)S(1)}, f32[128,512]{1,0:T(8,128)S(1)}, u32[]{:S(2)}, u32[]{:S(2)}) collective-permute-start(f32[128,512]{1,0:T(8,128)S(1)} %slice.38), channel_id=1, source_target_pairs={{1,0},{0,1},{129,128},{128,129},{3,2},{2,3},{131,130},{130,131},{5... | collective-permute-start | bytes 786440 | tf_op jit(solution)/shard_map/ppermute | solution.py:375
  168.3 2.8 %collective-permute-start.22 = (f32[256,512]{1,0:T(8,128)S(1)}, f32[256,512]{1,0:T(8,128)S(1)}, u32[]{:S(2)}, u32[]{:S(2)}) collective-permute-start(f32[256,512]{1,0:T(8,128)S(1)} %get-tuple-element.43.refs_5_), channel_id=1, source_target_pairs={{129,1},{1,129},{131,3},{3,131},{133,5},{5,133},{135,7},{7,135},{1... | collective-permute-start | bytes 1572872 | tf_op jit(solution)/shard_map/ppermute | solution.py:375
  171.1 0.0 collective-permute-done.19.other
  171.1 17.0 %cholesky.1 = (f32[512,512]{1,0:T(8,128)}, f32[512,512]{1,0:T(8,128)S(1)}) custom-call(f32[5,128,128]{2,1,0:T(8,128)S(1)} %bitcast.32, f32[5,128,128]{2,1,0:T(8,128)S(1)} %collective-permute-done.19.other), custom_call_target="tpu_custom_call" | custom-call | flops 17179869184 | bytes 4194304 | tf_op jit(solution)/shard_map/cholesky/pallas_call | solution.py:313
  188.0 0.0 collective-permute-done.21.refs_3_
  188.0 0.0 collective-permute-done.20.refs_2_
  188.0 0.0 collective-permute-done.22.refs_7_
  188.1 2.8 %basis.1 = f32[2048,256]{1,0:T(8,128)} custom-call(f32[512,512]{1,0:T(8,128)S(1)} %get-tuple-element.37.inverse, f32[256,512]{1,0:T(8,128)S(1)} %get-tuple-element.32.refs_0_, f32[256,512]{1,0:T(8,128)S(1)} %collective-permute-done.15.refs_1_, f32[128,512]{1,0:T(8,128)S(1)} %collective-permute-done.20.refs_2_, ...), custom_call_target="tpu_custom_call" | custom-call | tf_op jit(solution)/shard_map/basis/pallas_call | solution.py:354
  (14 shorter events, 0.2 us)
Async XLA Ops:
  0.6 75.8 %copy-start.4 = (s32[1,1,4]{2,1,0:T(1,128)S(1)}, s32[1,1,4]{2,1,0:T(1,128)}, u32[]{:S(2)}) copy-start(s32[1,1,4]{2,1,0:T(1,128)} %param.7) | copy-start | bytes 52
  0.6 75.8 %copy-start.2 = (s32[1,1,4]{2,1,0:T(1,128)S(1)}, s32[1,1,4]{2,1,0:T(1,128)}, u32[]{:S(2)}) copy-start(s32[1,1,4]{2,1,0:T(1,128)} %param.6) | copy-start | bytes 52
  1.3 1.2 copy-start
  2.5 0.7 copy-start.1
  3.2 0.7 copy-start.3
  8.3 2.7 %collective-permute-start = (f32[4,2,256,128]{3,2,1,0:T(8,128)S(1)}, f32[4,2,256,128]{3,2,1,0:T(8,128)S(1)}, u32[]{:S(2)}, u32[]{:S(2)}) collective-permute-start(f32[4,2,256,128]{3,2,1,0:T(8,128)S(1)} %get-tuple-element.25), channel_id=1, source_target_pairs={{0,2},{2,0},{1,3},{3,1},{4,6},{6,4},{5,7},{7,5},{8,10},{10,8},{9,1... | collective-permute-start | bytes 3145736 | tf_op jit(solution)/shard_map/ppermute | solution.py:366
  11.1 9.6 %collective-permute-start.1 = (f32[2,256,128]{2,1,0:T(8,128)S(1)}, f32[2,256,128]{2,1,0:T(8,128)S(1)}, u32[]{:S(2)}, u32[]{:S(2)}) collective-permute-start(f32[2,256,128]{2,1,0:T(8,128)S(1)} %get-tuple-element.46), channel_id=1, source_target_pairs={{0,4},{4,8},{8,12},{12,0},{1,5},{5,9},{9,13},{13,1},{2,6},{6,10},{... | collective-permute-start | bytes 786440 | tf_op jit(solution)/shard_map/ppermute | solution.py:371
  12.8 14.5 %collective-permute-start.3 = (f32[2,256,128]{2,1,0:T(8,128)S(1)}, f32[2,256,128]{2,1,0:T(8,128)S(1)}, u32[]{:S(2)}, u32[]{:S(2)}) collective-permute-start(f32[2,256,128]{2,1,0:T(8,128)S(1)} %get-tuple-element.47), channel_id=1, source_target_pairs={{0,8},{4,12},{8,0},{12,4},{1,9},{5,13},{9,1},{13,5},{2,10},{6,14},... | collective-permute-start | bytes 786440 | tf_op jit(solution)/shard_map/ppermute | solution.py:371
  15.3 12.0 %collective-permute-start.2 = (f32[2,256,128]{2,1,0:T(8,128)S(1)}, f32[2,256,128]{2,1,0:T(8,128)S(1)}, u32[]{:S(2)}, u32[]{:S(2)}) collective-permute-start(f32[2,256,128]{2,1,0:T(8,128)S(1)} %get-tuple-element.48), channel_id=1, source_target_pairs={{0,12},{4,0},{8,4},{12,8},{1,13},{5,1},{9,5},{13,9},{2,14},{6,2},{... | collective-permute-start | bytes 786440 | tf_op jit(solution)/shard_map/ppermute | solution.py:371
  59.9 11.6 %collective-permute-start.6 = (f32[2,256,128]{2,1,0:T(8,128)S(1)}, f32[2,256,128]{2,1,0:T(8,128)S(1)}, u32[]{:S(2)}, u32[]{:S(2)}) collective-permute-start(f32[2,256,128]{2,1,0:T(8,128)S(1)} %bitcast.26), channel_id=1, source_target_pairs={{0,12},{4,0},{8,4},{12,8},{1,13},{5,1},{9,5},{13,9},{2,14},{6,2},{... | collective-permute-start | bytes 786440 | tf_op jit(solution)/shard_map/ppermute | solution.py:371
  63.2 9.4 %collective-permute-start.5 = (f32[2,256,128]{2,1,0:T(8,128)S(1)}, f32[2,256,128]{2,1,0:T(8,128)S(1)}, u32[]{:S(2)}, u32[]{:S(2)}) collective-permute-start(f32[2,256,128]{2,1,0:T(8,128)S(1)} %bitcast.27), channel_id=1, source_target_pairs={{0,8},{4,12},{8,0},{12,4},{1,9},{5,13},{9,1},{13,5},{2,10},{6,14},... | collective-permute-start | bytes 786440 | tf_op jit(solution)/shard_map/ppermute | solution.py:371
  63.2 11.7 %collective-permute-start.4 = (f32[2,256,128]{2,1,0:T(8,128)S(1)}, f32[2,256,128]{2,1,0:T(8,128)S(1)}, u32[]{:S(2)}, u32[]{:S(2)}) collective-permute-start(f32[2,256,128]{2,1,0:T(8,128)S(1)} %bitcast.28), channel_id=1, source_target_pairs={{0,4},{4,8},{8,12},{12,0},{1,5},{5,9},{9,13},{13,1},{2,6},{6,10},{... | collective-permute-start | bytes 786440 | tf_op jit(solution)/shard_map/ppermute | solution.py:371
  64.6 10.3 %collective-permute-start.7 = (f32[2,256,128]{2,1,0:T(8,128)S(1)}, f32[2,256,128]{2,1,0:T(8,128)S(1)}, u32[]{:S(2)}, u32[]{:S(2)}) collective-permute-start(f32[2,256,128]{2,1,0:T(8,128)S(1)} %bitcast.29), channel_id=1, source_target_pairs={{0,2},{2,0},{1,3},{3,1},{4,6},{6,4},{5,7},{7,5},{8,10},{10,8},{9,1... | collective-permute-start | bytes 786440 | tf_op jit(solution)/shard_map/ppermute | solution.py:366
  71.5 3.4 %collective-permute-start.10 = (f32[2,256,128]{2,1,0:T(8,128)S(1)}, f32[2,256,128]{2,1,0:T(8,128)S(1)}, u32[]{:S(2)}, u32[]{:S(2)}) collective-permute-start(f32[2,256,128]{2,1,0:T(8,128)S(1)} %collective-permute-done.6.rest_3_), channel_id=1, source_target_pairs={{0,2},{2,0},{1,3},{3,1},{4,6},{6,4},{5,7},{7,5},{8,10},{10,8},{9,1... | collective-permute-start | bytes 786440 | tf_op jit(solution)/shard_map/ppermute | solution.py:366
  72.6 2.4 %collective-permute-start.9 = (f32[2,256,128]{2,1,0:T(8,128)S(1)}, f32[2,256,128]{2,1,0:T(8,128)S(1)}, u32[]{:S(2)}, u32[]{:S(2)}) collective-permute-start(f32[2,256,128]{2,1,0:T(8,128)S(1)} %collective-permute-done.5.rest_2_), channel_id=1, source_target_pairs={{0,2},{2,0},{1,3},{3,1},{4,6},{6,4},{5,7},{7,5},{8,10},{10,8},{9,1... | collective-permute-start | bytes 786440 | tf_op jit(solution)/shard_map/ppermute | solution.py:366
  74.9 1.5 collective-permute-start.8
  81.2 14.9 %collective-permute-start.11 = (f32[4,256,128]{2,1,0:T(8,128)S(1)}, f32[4,256,128]{2,1,0:T(8,128)S(1)}, u32[]{:S(2)}, u32[]{:S(2)}) collective-permute-start(f32[4,256,128]{2,1,0:T(8,128)S(1)} %get-tuple-element.27), channel_id=1, source_target_pairs={{1,0},{0,1},{129,128},{128,129},{3,2},{2,3},{131,130},{130,131},{5... | collective-permute-start | bytes 1572872 | tf_op jit(solution)/shard_map/ppermute | solution.py:375
  81.8 26.2 %collective-permute-start.12 = (f32[4,256,128]{2,1,0:T(8,128)S(1)}, f32[4,256,128]{2,1,0:T(8,128)S(1)}, u32[]{:S(2)}, u32[]{:S(2)}) collective-permute-start(f32[4,256,128]{2,1,0:T(8,128)S(1)} %get-tuple-element.28), channel_id=1, source_target_pairs={{128,0},{129,1},{0,128},{1,129},{130,2},{131,3},{2,130},{3,131},{1... | collective-permute-start | bytes 1572872 | tf_op jit(solution)/shard_map/ppermute | solution.py:375
  85.1 24.2 %collective-permute-start.13 = (f32[4,256,128]{2,1,0:T(8,128)S(1)}, f32[4,256,128]{2,1,0:T(8,128)S(1)}, u32[]{:S(2)}, u32[]{:S(2)}) collective-permute-start(f32[4,256,128]{2,1,0:T(8,128)S(1)} %get-tuple-element.29), channel_id=1, source_target_pairs={{129,0},{128,1},{1,128},{0,129},{131,2},{130,3},{3,130},{2,131},{1... | collective-permute-start | bytes 1572872 | tf_op jit(solution)/shard_map/ppermute | solution.py:375
  113.1 3.5 %collective-permute-start.14 = (f32[5,128,128]{2,1,0:T(8,128)S(1)}, f32[5,128,128]{2,1,0:T(8,128)S(1)}, u32[]{:S(2)}, u32[]{:S(2)}) collective-permute-start(f32[5,128,128]{2,1,0:T(8,128)S(1)} %get-tuple-element.31), channel_id=1, source_target_pairs={{0,2},{2,0},{1,3},{3,1},{4,6},{6,4},{5,7},{7,5},{8,10},{10,8},{9,1... | collective-permute-start | bytes 983048 | tf_op jit(solution)/shard_map/ppermute | solution.py:366
  113.2 21.4 %collective-permute-start.16 = (f32[256,512]{1,0:T(8,128)S(1)}, f32[256,512]{1,0:T(8,128)S(1)}, u32[]{:S(2)}, u32[]{:S(2)}) collective-permute-start(f32[256,512]{1,0:T(8,128)S(1)} %get-tuple-element.32.refs_0_), channel_id=1, source_target_pairs={{129,0},{128,1},{1,128},{0,129},{131,2},{130,3},{3,130},{2,131},{1... | collective-permute-start | bytes 1572872 | tf_op jit(solution)/shard_map/ppermute | solution.py:375
  113.6 21.1 %collective-permute-start.15 = (f32[256,512]{1,0:T(8,128)S(1)}, f32[256,512]{1,0:T(8,128)S(1)}, u32[]{:S(2)}, u32[]{:S(2)}) collective-permute-start(f32[256,512]{1,0:T(8,128)S(1)} %get-tuple-element.32.refs_0_), channel_id=1, source_target_pairs={{1,0},{0,1},{129,128},{128,129},{3,2},{2,3},{131,130},{130,131},{5... | collective-permute-start | bytes 1572872 | tf_op jit(solution)/shard_map/ppermute | solution.py:375
  134.6 15.8 %collective-permute-start.18 = (f32[256,512]{1,0:T(8,128)S(1)}, f32[256,512]{1,0:T(8,128)S(1)}, u32[]{:S(2)}, u32[]{:S(2)}) collective-permute-start(f32[256,512]{1,0:T(8,128)S(1)} %get-tuple-element.43.refs_5_), channel_id=1, source_target_pairs={{128,1},{0,129},{130,3},{2,131},{132,5},{4,133},{134,7},{6,135},{1... | collective-permute-start | bytes 1572872 | tf_op jit(solution)/shard_map/ppermute | solution.py:375
  135.9 16.2 %collective-permute-start.17 = (f32[256,512]{1,0:T(8,128)S(1)}, f32[256,512]{1,0:T(8,128)S(1)}, u32[]{:S(2)}, u32[]{:S(2)}) collective-permute-start(f32[256,512]{1,0:T(8,128)S(1)} %get-tuple-element.43.refs_5_), channel_id=1, source_target_pairs={{0,1},{128,129},{2,3},{130,131},{4,5},{132,133},{6,7},{134,135},{8... | collective-permute-start | bytes 1572872 | tf_op jit(solution)/shard_map/ppermute | solution.py:375
  165.5 5.6 %collective-permute-start.19 = (f32[5,128,128]{2,1,0:T(8,128)S(1)}, f32[5,128,128]{2,1,0:T(8,128)S(1)}, u32[]{:S(2)}, u32[]{:S(2)}) collective-permute-start(f32[5,128,128]{2,1,0:T(8,128)S(1)} %bitcast.31), channel_id=1, source_target_pairs={{0,2},{2,0},{1,3},{3,1},{4,6},{6,4},{5,7},{7,5},{8,10},{10,8},{9,1... | collective-permute-start | bytes 983048 | tf_op jit(solution)/shard_map/ppermute | solution.py:366
  165.5 22.5 %collective-permute-start.21 = (f32[128,512]{1,0:T(8,128)S(1)}, f32[128,512]{1,0:T(8,128)S(1)}, u32[]{:S(2)}, u32[]{:S(2)}) collective-permute-start(f32[128,512]{1,0:T(8,128)S(1)} %slice.39), channel_id=1, source_target_pairs={{129,0},{128,1},{1,128},{0,129},{131,2},{130,3},{3,130},{2,131},{1... | collective-permute-start | bytes 786440 | tf_op jit(solution)/shard_map/ppermute | solution.py:375
  166.3 21.8 %collective-permute-start.20 = (f32[128,512]{1,0:T(8,128)S(1)}, f32[128,512]{1,0:T(8,128)S(1)}, u32[]{:S(2)}, u32[]{:S(2)}) collective-permute-start(f32[128,512]{1,0:T(8,128)S(1)} %slice.38), channel_id=1, source_target_pairs={{1,0},{0,1},{129,128},{128,129},{3,2},{2,3},{131,130},{130,131},{5... | collective-permute-start | bytes 786440 | tf_op jit(solution)/shard_map/ppermute | solution.py:375
  168.3 19.8 %collective-permute-start.22 = (f32[256,512]{1,0:T(8,128)S(1)}, f32[256,512]{1,0:T(8,128)S(1)}, u32[]{:S(2)}, u32[]{:S(2)}) collective-permute-start(f32[256,512]{1,0:T(8,128)S(1)} %get-tuple-element.43.refs_5_), channel_id=1, source_target_pairs={{129,1},{1,129},{131,3},{3,131},{133,5},{5,133},{135,7},{7,135},{1... | collective-permute-start | bytes 1572872 | tf_op jit(solution)/shard_map/ppermute | solution.py:375
